TPU v7x, 128 devices: a whole 4x4x4 slice. The times are simulated.
128 devices in a mesh: gx: 8 (over y, core), gy: 16 (over x, z).
Axes of the slice: x: 4, y: 4, z: 4, core: 2. Of those that a mesh axis runs over, the one named last changes fastest.
Arguments:
- old_states: bfloat16 [16384, 12, 128], P(('gx', 'gy')), may hold values from -6 to 6
- weight_tiles: bfloat16 [49152, 128, 128], P(('gx', 'gy')), may hold values from -0.5 to 0.5
- source_block: int32 [98304], P(('gx', 'gy')), may hold values from 0 to 127
- tile_index: int32 [98304], P(('gx', 'gy')), may hold values from 0 to 383
- dest_device: int32 [98304], P(('gx', 'gy')), may hold values from 0 to 127, as said below
- dest_block: int32 [98304], P(('gx', 'gy')), may hold values from 0 to 255
- send_count: int32 [128], P(('gx', 'gy')), may hold values from 576 to 768, as said below
- velocity: float32 [2, 2048, 2048], P(None, 'gx', 'gy'), may hold values from -4 to 4
Outputs:
- new_states: float32 [2048, 12, 2048], P('gx', None, 'gy')
Inputs may be any that keep to these rules, and one draw needn't show every extreme that they name: `dest_device`: the live slots of a device name only the device itself and the devices of the tiles adjacent to its tile along gx and gy, diagonals included; among them no destination appears more than 192 times, and the device itself appears exactly 192 times. The live slots of a device are its first send_count slots; some device has all 768 live.
All inputs are finite; a program needn't handle non-finite values.
Results may differ from a plain program's by a relative error of at most 0.0033.
The roundings to bfloat16 on the way count: a program that leaves them out, or rounds other values in their place, can miss the bound.
Values may be sent and summed in bfloat16 or wider, within the bound.
A program may use at most 128 MiB of HBM per device.

v0:
```python
import jax
import jax.numpy as jnp
from jax import lax
from jax.sharding import PartitionSpec as P

time_step = 0.2
shape_factor = 0.95
interaction = 0.01
shear_modulus = 1.0
fiber_number = 2.0


def extended(x, sides, width):
    for axis, dim in sides:
        peers, length = (lax.axis_size(axis), x.shape[dim])
        up = [(i, (i + 1) % peers) for i in range(peers - 1)]
        down = [(j, i) for i, j in up]
        last = lax.slice_in_dim(x, length - width, length, axis=dim)
        initial = lax.slice_in_dim(x, 0, width, axis=dim)
        before = lax.ppermute(last, axis, up)
        after = lax.ppermute(initial, axis, down)
        x = jnp.concatenate([before, x, after], axis=dim)
    return x


def from_behind(value, axis, steps):
    count = lax.axis_size(axis)
    initial, last = (max(0, -steps), min(count, count - steps))
    return lax.ppermute(value, axis, [(source, source + steps) for source in range(initial, last)])


def product(left, right):
    return [
        [
            sum((left[first][inner] * right[inner][second] for inner in range(3)))
            for second in range(3)
        ]
        for first in range(3)
    ]


def advance(state_pad, flow_pad):
    centre = state_pad[1:-1, :, 1:-1]
    flow_x = flow_pad[0, 1:-1, 1:-1]
    flow_y = flow_pad[1, 1:-1, 1:-1]
    grad_xx = 0.5 * (flow_pad[0, 2:, 1:-1] - flow_pad[0, :-2, 1:-1])
    grad_xy = 0.5 * (flow_pad[0, 1:-1, 2:] - flow_pad[0, 1:-1, :-2])
    grad_yx = 0.5 * (flow_pad[1, 2:, 1:-1] - flow_pad[1, :-2, 1:-1])
    grad_yy = 0.5 * (flow_pad[1, 1:-1, 2:] - flow_pad[1, 1:-1, :-2])
    grad_zz = -(grad_xx + grad_yy)
    strain_xy = 0.5 * (grad_xy + grad_yx)
    spin_xy = 0.5 * (grad_xy - grad_yx)
    upwind = (
        jnp.maximum(flow_x, 0.0)[:, None, :] * (centre - state_pad[:-2, :, 1:-1])
        + jnp.minimum(flow_x, 0.0)[:, None, :] * (state_pad[2:, :, 1:-1] - centre)
        + jnp.maximum(flow_y, 0.0)[:, None, :] * (centre - state_pad[1:-1, :, :-2])
        + jnp.minimum(flow_y, 0.0)[:, None, :] * (state_pad[1:-1, :, 2:] - centre)
    )
    parts = [centre[:, index, :] for index in range(6)]
    orient = [
        [parts[0], parts[3], parts[4]],
        [parts[3], parts[1], parts[5]],
        [parts[4], parts[5], parts[2]],
    ]
    zero = jnp.zeros_like(grad_xx)
    rate = [[grad_xx, strain_xy, zero], [strain_xy, grad_yy, zero], [zero, zero, grad_zz]]
    spin = [[zero, spin_xy, zero], [-spin_xy, zero, zero], [zero, zero, zero]]
    contraction = sum(
        (orient[first][second] * rate[first][second] for first in range(3) for second in range(3))
    )
    shear = jnp.sqrt(
        2.0
        * sum(
            (rate[first][second] * rate[first][second] for first in range(3) for second in range(3))
        )
        + 1.0
    )
    spin_orient = product(spin, orient)
    orient_spin = product(orient, spin)
    rate_orient = product(rate, orient)
    orient_rate = product(orient, rate)
    sources = []
    for first, second in ((0, 0), (1, 1), (2, 2), (0, 1), (0, 2), (1, 2)):
        delta = 1.0 if first == second else 0.0
        sources.append(
            spin_orient[first][second]
            - orient_spin[first][second]
            + shape_factor
            * (
                rate_orient[first][second]
                + orient_rate[first][second]
                - 2.0 * contraction * orient[first][second]
            )
            + 2.0 * interaction * shear * (delta - 3.0 * orient[first][second])
        )
    sources = sources + [grad_xx, grad_yy, strain_xy]
    for first, second in ((0, 0), (1, 1), (0, 1)):
        sources.append(
            2.0
            * shear_modulus
            * (rate[first][second] + fiber_number * contraction * orient[first][second])
        )
    source = jnp.stack(sources, axis=1)
    return centre + time_step * (source - upwind)


def per_device(
    old_states,
    weight_tiles,
    source_block,
    tile_index,
    dest_device,
    dest_block,
    send_count,
    velocity,
):
    flow_pad = extended(velocity, (("gx", 1), ("gy", 2)), 1)
    slot_count = source_block.shape[0]
    block_count = old_states.shape[0]
    state_count = old_states.shape[1]
    lane_count = old_states.shape[2]
    tile_rows = velocity.shape[1]
    block_onehot = (source_block[:, None] == jnp.arange(block_count)[None, :]).astype(jnp.bfloat16)
    block_pick = jnp.dot(
        block_onehot,
        old_states.reshape(block_count, state_count * lane_count),
        preferred_element_type=jnp.float32,
    )
    block_pick = block_pick.astype(jnp.bfloat16).reshape(slot_count, state_count, lane_count)
    tile_pick = weight_tiles[tile_index]
    pieces = jnp.einsum("snk,sck->scn", tile_pick, block_pick, preferred_element_type=jnp.float32)
    is_live = jnp.arange(slot_count) < send_count[0]
    pieces = jnp.where(is_live[:, None, None], pieces, 0.0).astype(jnp.bfloat16)
    width_y = lax.axis_size("gy")
    capacity = slot_count // 4
    own_x = lax.axis_index("gx")
    own_y = lax.axis_index("gy")
    step_x = dest_device // width_y - own_x
    step_y = dest_device % width_y - own_y
    direction = (step_x + 1) * 3 + (step_y + 1)
    matches = ((direction[:, None] == jnp.arange(9)[None, :]) & is_live[:, None]).astype(jnp.int32)
    earlier = jnp.cumsum(matches, axis=0) - matches
    position = jnp.sum(earlier * matches, axis=1)
    target = jnp.where(is_live, direction * capacity + position, 9 * capacity)
    placing = target[None, :] == jnp.arange(9 * capacity)[:, None]
    outgoing = jnp.dot(
        placing.astype(jnp.bfloat16),
        pieces.reshape(slot_count, state_count * lane_count),
        preferred_element_type=jnp.float32,
    )
    outgoing = outgoing.astype(jnp.bfloat16).reshape(3, 3, capacity, state_count, lane_count)
    labels = jnp.sum(jnp.where(placing, dest_block[None, :], 0), axis=1)
    labels = labels.reshape(3, 3, capacity)
    received = [outgoing[1, 1]]
    received_ids = [labels[1, 1]]
    for move_x in (-1, 0, 1):
        for move_y in (-1, 0, 1):
            if move_x != 0 or move_y != 0:
                got, got_ids = from_behind(
                    (outgoing[move_x + 1, move_y + 1], labels[move_x + 1, move_y + 1]),
                    ("gx", "gy"),
                    move_x * width_y + move_y,
                )
                received.append(got)
                received_ids.append(got_ids)
    arrived_rows = jnp.concatenate(received, axis=0).reshape(-1, state_count * lane_count)
    arrived_ids = jnp.concatenate(received_ids, axis=0)
    selector = (jnp.arange(tile_rows)[:, None] == arrived_ids[None, :]).astype(jnp.bfloat16)
    remapped = jnp.dot(selector, arrived_rows, preferred_element_type=jnp.float32).reshape(
        tile_rows, state_count, lane_count
    )
    state_pad = extended(remapped, (("gx", 0), ("gy", 2)), 1)
    return advance(state_pad, flow_pad)


def solution(mesh):
    in_specs = (
        P(("gx", "gy"), None, None),
        P(("gx", "gy"), None, None),
        P(("gx", "gy")),
        P(("gx", "gy")),
        P(("gx", "gy")),
        P(("gx", "gy")),
        P(("gx", "gy")),
        P(None, "gx", "gy"),
    )
    out_specs = P("gx", None, "gy")
    return jax.shard_map(
        per_device, mesh=mesh, in_specs=in_specs, out_specs=out_specs, check_vma=False
    )
```

profile of v0, /device:TPU:10, one launch (start us, length us, event | category | flops | bytes accessed | tf_op | source)
XLA Modules:
  0.0 233.7 jit_solution(8672716387181893651)
XLA Ops:
  4.1 2.5 %copy.121 = bf16[768,1536]{0,1:T(8,128)(2,1)} copy(bf16[768,1536]{1,0:T(8,128)(2,1)S(1)} %convolution_convert_fusion.1) | data formatting | bytes 4718592 | tf_op jit(solution)/shard_map/convert_element_type | solution.py:129
  6.6 5.0 %copy.122 = bf16[768,12,128]{2,1,0:T(8,128)(2,1)} copy(bf16[768,12,128]{0,2,1:T(8,128)(2,1)} %bitcast.251) | data formatting | bytes 4718592 | tf_op jit(solution)/shard_map/reshape | solution.py:129
  12.3 23.9 %gather_fusion = bf16[768,128,128]{2,1,0:T(8,128)(2,1)} fusion(bf16[384,128,128]{2,1,0:T(8,128)(2,1)} %param.9, s32[1024]{0:T(1024)S(1)} %pad_clamp_fusion), kind=kCustom, calls=%fused_computation | custom fusion | bytes 50334720 | tf_op jit(solution)/shard_map/gather | solution.py:130
  36.1 18.4 %fusion.104 = bf16[768,12,128]{2,1,0:T(8,128)(2,1)S(1)} fusion(bf16[768,12,128]{2,1,0:T(8,128)(2,1)} %copy.122, bf16[768,128,128]{2,1,0:T(8,128)(2,1)} %gather_fusion), kind=kOutput, calls=%fused_computation.208 | convolution fusion | flops 301989888 | bytes 29884416 | tf_op jit(solution)/shard_map/snk,sck->scn/dot_general | solution.py:131
  54.5 2.3 fusion
  56.7 2.8 %copy.124 = bf16[768,12,128]{0,2,1:T(8,128)(2,1)S(1)} copy(bf16[768,12,128]{2,0,1:T(8,128)(2,1)} %fusion) | data formatting | bytes 4718592 | tf_op jit(solution)/shard_map/convert_element_type | solution.py:133
  61.8 6.1 %convolution_convert_fusion = bf16[1728,1536]{1,0:T(8,128)(2,1)} fusion(bf16[768,1536]{0,1:T(8,128)(2,1)S(1)} %bitcast.253, s32[768]{0:T(1024)S(1)} %add_select_fusion.2), kind=kOutput, calls=%fused_computation.1 | convolution fusion | flops 4080844800 | bytes 7670784 | tf_op jit(solution)/shard_map/dot_general | solution.py:146
  67.9 10.4 %reshape.385 = bf16[3,3,192,12,128]{4,3,2,1,0:T(8,128)(2,1)} reshape(bf16[1728,1536]{1,0:T(8,128)(2,1)} %convolution_convert_fusion) | data formatting | bytes 10616832 | tf_op jit(solution)/shard_map/reshape | solution.py:151
  78.4 5.7 %slice_bitcast_fusion = (bf16[192,12,128]{2,1,0:T(8,128)(2,1)S(1)}, bf16[192,12,128]{2,1,0:T(8,128)(2,1)S(1)}, bf16[192,12,128]{2,1,0:T(8,128)(2,1)S(1)}, bf16[1...) fusion(bf16[3,3,192,12,128]{4,3,2,1,0:T(8,128)(2,1)} %reshape.385), kind=kLoop, calls=%fused_computation.33 | loop fusion | bytes 10616832 | tf_op jit(solution)/shard_map/squeeze | solution.py:160
  85.0 5.4 %collective-permute-start.8 = (bf16[192,12,128]{2,0,1:T(8,128)(2,1)}, bf16[192,12,128]{2,0,1:T(8,128)(2,1)}, u32[]{:S(2)}, u32[]{:S(2)}) collective-permute-start(bf16[192,12,128]{2,0,1:T(8,128)(2,1)} %copy.125), channel_id=1, source_target_pairs={{17,0},{18,1},{19,2},{20,3},{21,4},{22,5},{23,6},{24,7},{25,8},{26... | collective-permute-start | bytes 1769480 | tf_op jit(solution)/shard_map/ppermute | solution.py:29
  91.7 2.6 %collective-permute-start = (s32[192]{0:T(256)S(1)}, s32[192]{0:T(256)S(1)}, u32[]{:S(2)}, u32[]{:S(2)}) collective-permute-start(s32[192]{0:T(256)S(1)} %bitcast.264), channel_id=1, source_target_pairs={{17,0},{18,1},{19,2},{20,3},{21,4},{22,5},{23,6},{24,7},{25,8},{26... | collective-permute-start | bytes 2312 | tf_op jit(solution)/shard_map/ppermute | solution.py:29
  96.6 2.3 collective-permute-start.16
  99.0 3.3 %collective-permute-start.17 = (f32[2,1,128]{1,2,0:T(8,128)S(1)}, f32[2,1,128]{1,2,0:T(8,128)S(1)}, u32[]{:S(2)}, u32[]{:S(2)}) collective-permute-start(f32[2,1,128]{1,2,0:T(8,128)S(1)} %copy.143), channel_id=1, source_target_pairs={{16,0},{32,16},{48,32},{64,48},{80,64},{96,80},{112,96},{17,1},{33... | collective-permute-start | bytes 3080 | tf_op jit(solution)/shard_map/ppermute | solution.py:21
  102.3 2.1 bitcast_dynamic-update-slice_fusion
  104.5 3.0 %collective-permute-start.2 = (s32[192]{0:T(256)S(1)}, s32[192]{0:T(256)S(1)}, u32[]{:S(2)}, u32[]{:S(2)}) collective-permute-start(s32[192]{0:T(256)S(1)} %bitcast.262), channel_id=1, source_target_pairs={{15,0},{16,1},{17,2},{18,3},{19,4},{20,5},{21,6},{22,7},{23,8},{24... | collective-permute-start | bytes 2312 | tf_op jit(solution)/shard_map/ppermute | solution.py:29
  107.5 4.6 %collective-permute-start.3 = (s32[192]{0:T(256)S(1)}, s32[192]{0:T(256)S(1)}, u32[]{:S(2)}, u32[]{:S(2)}) collective-permute-start(s32[192]{0:T(256)S(1)} %bitcast.261), channel_id=1, source_target_pairs={{1,0},{2,1},{3,2},{4,3},{5,4},{6,5},{7,6},{8,7},{9,8},{10,9},{11,1... | collective-permute-start | bytes 2312 | tf_op jit(solution)/shard_map/ppermute | solution.py:29
  114.7 5.7 %collective-permute-start.5 = (s32[192]{0:T(256)S(1)}, s32[192]{0:T(256)S(1)}, u32[]{:S(2)}, u32[]{:S(2)}) collective-permute-start(s32[192]{0:T(256)S(1)} %bitcast.259), channel_id=1, source_target_pairs={{0,15},{1,16},{2,17},{3,18},{4,19},{5,20},{6,21},{7,22},{8,23},{9,... | collective-permute-start | bytes 2312 | tf_op jit(solution)/shard_map/ppermute | solution.py:29
  123.0 6.0 %collective-permute-start.18 = (f32[2,258,1]{1,2,0:T(1,128)S(1)}, f32[2,258,1]{1,2,0:T(1,128)S(1)}, u32[]{:S(2)}, u32[]{:S(2)}) collective-permute-start(f32[2,258,1]{1,2,0:T(1,128)S(1)} %get-tuple-element.26), channel_id=1, source_target_pairs={{1,0},{2,1},{3,2},{4,3},{5,4},{6,5},{7,6},{8,7},{9,8},{10,9},{11,1... | collective-permute-start | bytes 6200 | tf_op jit(solution)/shard_map/ppermute | solution.py:21
  129.8 2.2 copy.127
  135.0 2.8 %collective-permute-start.6 = (s32[192]{0:T(256)}, s32[192]{0:T(256)}, u32[]{:S(2)}, u32[]{:S(2)}) collective-permute-start(s32[192]{0:T(256)} %bitcast.10), channel_id=1, source_target_pairs={{0,16},{1,17},{2,18},{3,19},{4,20},{5,21},{6,22},{7,23},{8,24},{9,... | collective-permute-start | bytes 2312 | tf_op jit(solution)/shard_map/ppermute | solution.py:29
  145.1 2.8 %collective-permute-start.9 = (bf16[192,12,128]{2,0,1:T(8,128)(2,1)}, bf16[192,12,128]{2,0,1:T(8,128)(2,1)S(1)}, u32[]{:S(2)}, u32[]{:S(2)}) collective-permute-start(bf16[192,12,128]{2,0,1:T(8,128)(2,1)} %copy.127), channel_id=1, source_target_pairs={{16,0},{17,1},{18,2},{19,3},{20,4},{21,5},{22,6},{23,7},{24,8},{25... | collective-permute-start | bytes 1769480 | tf_op jit(solution)/shard_map/ppermute | solution.py:29
  150.6 6.5 %collective-permute-start.11 = (bf16[192,12,128]{2,0,1:T(8,128)(2,1)}, bf16[192,12,128]{2,0,1:T(8,128)(2,1)S(1)}, u32[]{:S(2)}, u32[]{:S(2)}) collective-permute-start(bf16[192,12,128]{2,0,1:T(8,128)(2,1)} %copy.131), channel_id=1, source_target_pairs={{1,0},{2,1},{3,2},{4,3},{5,4},{6,5},{7,6},{8,7},{9,8},{10,9},{11,1... | collective-permute-start | bytes 1769480 | tf_op jit(solution)/shard_map/ppermute | solution.py:29
  159.3 5.0 %collective-permute-start.13 = (bf16[192,12,128]{2,0,1:T(8,128)(2,1)}, bf16[192,12,128]{2,0,1:T(8,128)(2,1)S(1)}, u32[]{:S(2)}, u32[]{:S(2)}) collective-permute-start(bf16[192,12,128]{2,0,1:T(8,128)(2,1)} %copy.135), channel_id=1, source_target_pairs={{0,15},{1,16},{2,17},{3,18},{4,19},{5,20},{6,21},{7,22},{8,23},{9,... | collective-permute-start | bytes 1769480 | tf_op jit(solution)/shard_map/ppermute | solution.py:29
  166.3 4.0 %collective-permute-start.14 = (bf16[192,12,128]{2,0,1:T(8,128)(2,1)}, bf16[192,12,128]{2,0,1:T(8,128)(2,1)S(1)}, u32[]{:S(2)}, u32[]{:S(2)}) collective-permute-start(bf16[192,12,128]{2,0,1:T(8,128)(2,1)} %copy.137), channel_id=1, source_target_pairs={{0,16},{1,17},{2,18},{3,19},{4,20},{5,21},{6,22},{7,23},{8,24},{9,... | collective-permute-start | bytes 1769480 | tf_op jit(solution)/shard_map/ppermute | solution.py:29
  175.7 6.0 %collective-permute-done.12 = bf16[192,12,128]{2,0,1:T(8,128)(2,1)S(1)} collective-permute-done((bf16[192,12,128]{2,0,1:T(8,128)(2,1)}, bf16[192,12,128]{2,0,1:T(8,128)(2,1)S(1)}, u32[]{:S(2)}, u32[]{:S(2)}) %collective-permute-start.12) | collective-permute-done | bytes 589856 | tf_op jit(solution)/shard_map/ppermute | solution.py:29
  185.3 8.4 %collective-permute-done.15 = bf16[192,12,128]{2,0,1:T(8,128)(2,1)S(1)} collective-permute-done((bf16[192,12,128]{2,0,1:T(8,128)(2,1)S(1)}, bf16[192,12,128]{2,0,1:T(8,128)(2,1)S(1)}, u32[]{:S(2)}, u32[]{:S(2)}) %collective-permute-start.15) | collective-permute-done | bytes 589856 | tf_op jit(solution)/shard_map/ppermute | solution.py:29
  194.7 5.2 %fusion.2 = f32[256,1536]{1,0:T(8,128)} fusion(bf16[1728,1536]{1,0:T(8,128)(2,1)} %bitcast_dynamic-update-slice_fusion.1, s32[1728]{0:T(1024)S(1)} %concatenate.61), kind=kOutput, calls=%fused_computation.9 | convolution fusion | flops 1359396864 | bytes 6888192 | tf_op jit(solution)/shard_map/dot_general | solution.py:169
  206.0 2.4 %collective-permute-start.20 = (f32[1,12,128]{2,0,1:T(1,128)S(1)}, f32[1,12,128]{2,0,1:T(1,128)S(1)}, u32[]{:S(2)}, u32[]{:S(2)}) collective-permute-start(f32[1,12,128]{2,0,1:T(1,128)S(1)} %get-tuple-element.22), channel_id=1, source_target_pairs={{0,16},{16,32},{32,48},{48,64},{64,80},{80,96},{96,112},{1,17},{17... | collective-permute-start | bytes 18440 | tf_op jit(solution)/shard_map/ppermute | solution.py:20
  211.5 8.4 %collective-permute-start.23 = (f32[258,12,1]{0,2,1:T(1,128)S(1)}, f32[258,12,1]{0,2,1:T(1,128)S(1)}, u32[]{:S(2)}, u32[]{:S(2)}) collective-permute-start(f32[258,12,1]{0,2,1:T(1,128)S(1)} %get-tuple-element.21), channel_id=1, source_target_pairs={{1,0},{2,1},{3,2},{4,3},{5,4},{6,5},{7,6},{8,7},{9,8},{10,9},{11,1... | collective-permute-start | bytes 37160 | tf_op jit(solution)/shard_map/ppermute | solution.py:21
  221.9 5.8 %collective-permute-done.22 = f32[258,12,1]{0,2,1:T(1,128)S(1)} collective-permute-done((f32[258,12,1]{0,2,1:T(1,128)S(1)}, f32[258,12,1]{0,2,1:T(1,128)S(1)}, u32[]{:S(2)}, u32[]{:S(2)}) %collective-permute-start.22) | collective-permute-done | bytes 12416 | tf_op jit(solution)/shard_map/ppermute | solution.py:20
  227.7 3.0 %fusion.8 = f32[256,12,128]{0,2,1:T(8,128)} fusion(f32[256,12,128]{0,2,1:T(8,128)S(1)} %bitcast.250, f32[256,12,128]{0,2,1:T(8,128)S(1)} %fusion.60, f32[258,12,1]{0,2,1:T(1,128)S(1)} %collective-permute-done.23, f32[1,12,128]{0,2,1:T(8,128)S(1)} %copy.152, f32[1,12,128]{0,2,1:T(8,128)S(1)} %copy.149, f32[258,12,1]{0,2,1:T(1,128)S(1)} %collective-permute-done.22, ...), kind=kLoop, calls=%fused_computation.16 | loop fusion | flops 8650752 | bytes 5279936 | tf_op jit(solution)/shard_map/add | solution.py:104
  230.7 3.0 %copy.157 = f32[256,12,128]{2,0,1:T(8,128)} copy(f32[256,12,128]{0,2,1:T(8,128)} %fusion.8) | data formatting | bytes 3145728 | tf_op jit(solution)/shard_map/add | solution.py:104
  (145 shorter events, 54.9 us)
Async XLA Ops:
  78.4 18.1 %copy-start.5 = (f32[2,256,128]{2,1,0:T(8,128)S(1)}, f32[2,256,128]{2,1,0:T(8,128)}, u32[]{:S(2)}) copy-start(f32[2,256,128]{2,1,0:T(8,128)} %param.15) | copy-start | bytes 786436
  85.0 74.2 %collective-permute-start.8 = (bf16[192,12,128]{2,0,1:T(8,128)(2,1)}, bf16[192,12,128]{2,0,1:T(8,128)(2,1)}, u32[]{:S(2)}, u32[]{:S(2)}) collective-permute-start(bf16[192,12,128]{2,0,1:T(8,128)(2,1)} %copy.125), channel_id=1, source_target_pairs={{17,0},{18,1},{19,2},{20,3},{21,4},{22,5},{23,6},{24,7},{25,8},{26... | collective-permute-start | bytes 1769480 | tf_op jit(solution)/shard_map/ppermute | solution.py:29
  91.7 21.0 %collective-permute-start = (s32[192]{0:T(256)S(1)}, s32[192]{0:T(256)S(1)}, u32[]{:S(2)}, u32[]{:S(2)}) collective-permute-start(s32[192]{0:T(256)S(1)} %bitcast.264), channel_id=1, source_target_pairs={{17,0},{18,1},{19,2},{20,3},{21,4},{22,5},{23,6},{24,7},{25,8},{26... | collective-permute-start | bytes 2312 | tf_op jit(solution)/shard_map/ppermute | solution.py:29
  94.3 20.4 %collective-permute-start.1 = (s32[192]{0:T(256)S(1)}, s32[192]{0:T(256)S(1)}, u32[]{:S(2)}, u32[]{:S(2)}) collective-permute-start(s32[192]{0:T(256)S(1)} %bitcast.263), channel_id=1, source_target_pairs={{16,0},{17,1},{18,2},{19,3},{20,4},{21,5},{22,6},{23,7},{24,8},{25... | collective-permute-start | bytes 2312 | tf_op jit(solution)/shard_map/ppermute | solution.py:29
  96.6 7.9 %collective-permute-start.16 = (f32[2,1,128]{1,2,0:T(8,128)S(1)}, f32[2,1,128]{1,2,0:T(8,128)S(1)}, u32[]{:S(2)}, u32[]{:S(2)}) collective-permute-start(f32[2,1,128]{1,2,0:T(8,128)S(1)} %copy.142), channel_id=1, source_target_pairs={{0,16},{16,32},{32,48},{48,64},{64,80},{80,96},{96,112},{1,17},{17... | collective-permute-start | bytes 3080 | tf_op jit(solution)/shard_map/ppermute | solution.py:20
  99.0 8.5 %collective-permute-start.17 = (f32[2,1,128]{1,2,0:T(8,128)S(1)}, f32[2,1,128]{1,2,0:T(8,128)S(1)}, u32[]{:S(2)}, u32[]{:S(2)}) collective-permute-start(f32[2,1,128]{1,2,0:T(8,128)S(1)} %copy.143), channel_id=1, source_target_pairs={{16,0},{32,16},{48,32},{64,48},{80,64},{96,80},{112,96},{17,1},{33... | collective-permute-start | bytes 3080 | tf_op jit(solution)/shard_map/ppermute | solution.py:21
  104.5 27.5 %copy-start.2 = (bf16[192,12,128]{2,1,0:T(8,128)(2,1)S(1)}, bf16[192,12,128]{2,1,0:T(8,128)(2,1)}, u32[]{:S(2)}) copy-start(bf16[192,12,128]{2,1,0:T(8,128)(2,1)} %get-tuple-element.16) | copy-start | bytes 1769476
  104.5 15.9 %collective-permute-start.2 = (s32[192]{0:T(256)S(1)}, s32[192]{0:T(256)S(1)}, u32[]{:S(2)}, u32[]{:S(2)}) collective-permute-start(s32[192]{0:T(256)S(1)} %bitcast.262), channel_id=1, source_target_pairs={{15,0},{16,1},{17,2},{18,3},{19,4},{20,5},{21,6},{22,7},{23,8},{24... | collective-permute-start | bytes 2312 | tf_op jit(solution)/shard_map/ppermute | solution.py:29
  107.5 14.9 %collective-permute-start.3 = (s32[192]{0:T(256)S(1)}, s32[192]{0:T(256)S(1)}, u32[]{:S(2)}, u32[]{:S(2)}) collective-permute-start(s32[192]{0:T(256)S(1)} %bitcast.261), channel_id=1, source_target_pairs={{1,0},{2,1},{3,2},{4,3},{5,4},{6,5},{7,6},{8,7},{9,8},{10,9},{11,1... | collective-permute-start | bytes 2312 | tf_op jit(solution)/shard_map/ppermute | solution.py:29
  112.8 20.2 %copy-start.15 = (s32[192]{0:T(256)}, s32[192]{0:T(256)S(1)}, u32[]{:S(2)}) copy-start(s32[192]{0:T(256)S(1)} %collective-permute-done) | copy-start | bytes 2308
  112.8 22.2 %collective-permute-start.4 = (s32[192]{0:T(256)S(1)}, s32[192]{0:T(256)S(1)}, u32[]{:S(2)}, u32[]{:S(2)}) collective-permute-start(s32[192]{0:T(256)S(1)} %bitcast.260), channel_id=1, source_target_pairs={{0,1},{1,2},{2,3},{3,4},{4,5},{5,6},{6,7},{7,8},{8,9},{9,10},{10,1... | collective-permute-start | bytes 2312 | tf_op jit(solution)/shard_map/ppermute | solution.py:29
  114.7 18.3 %copy-start.17 = (s32[192]{0:T(256)}, s32[192]{0:T(256)S(1)}, u32[]{:S(2)}) copy-start(s32[192]{0:T(256)S(1)} %collective-permute-done.1) | copy-start | bytes 2308
  114.7 23.1 %collective-permute-start.5 = (s32[192]{0:T(256)S(1)}, s32[192]{0:T(256)S(1)}, u32[]{:S(2)}, u32[]{:S(2)}) collective-permute-start(s32[192]{0:T(256)S(1)} %bitcast.259), channel_id=1, source_target_pairs={{0,15},{1,16},{2,17},{3,18},{4,19},{5,20},{6,21},{7,22},{8,23},{9,... | collective-permute-start | bytes 2312 | tf_op jit(solution)/shard_map/ppermute | solution.py:29
  120.5 30.1 %collective-permute-start.19 = (f32[2,258,1]{1,2,0:T(1,128)}, f32[2,258,1]{1,2,0:T(1,128)S(1)}, u32[]{:S(2)}, u32[]{:S(2)}) collective-permute-start(f32[2,258,1]{1,2,0:T(1,128)} %get-tuple-element.27), channel_id=1, source_target_pairs={{0,1},{1,2},{2,3},{3,4},{4,5},{5,6},{6,7},{7,8},{8,9},{9,10},{10,1... | collective-permute-start | bytes 6200 | tf_op jit(solution)/shard_map/ppermute | solution.py:20
  123.0 34.1 %collective-permute-start.18 = (f32[2,258,1]{1,2,0:T(1,128)S(1)}, f32[2,258,1]{1,2,0:T(1,128)S(1)}, u32[]{:S(2)}, u32[]{:S(2)}) collective-permute-start(f32[2,258,1]{1,2,0:T(1,128)S(1)} %get-tuple-element.26), channel_id=1, source_target_pairs={{1,0},{2,1},{3,2},{4,3},{5,4},{6,5},{7,6},{8,7},{9,8},{10,9},{11,1... | collective-permute-start | bytes 6200 | tf_op jit(solution)/shard_map/ppermute | solution.py:21
  135.0 10.1 %collective-permute-start.6 = (s32[192]{0:T(256)}, s32[192]{0:T(256)}, u32[]{:S(2)}, u32[]{:S(2)}) collective-permute-start(s32[192]{0:T(256)} %bitcast.10), channel_id=1, source_target_pairs={{0,16},{1,17},{2,18},{3,19},{4,20},{5,21},{6,22},{7,23},{8,24},{9,... | collective-permute-start | bytes 2312 | tf_op jit(solution)/shard_map/ppermute | solution.py:29
  137.8 10.1 %collective-permute-start.7 = (s32[192]{0:T(256)}, s32[192]{0:T(256)}, u32[]{:S(2)}, u32[]{:S(2)}) collective-permute-start(s32[192]{0:T(256)} %bitcast.11), channel_id=1, source_target_pairs={{0,17},{1,18},{2,19},{3,20},{4,21},{5,22},{6,23},{7,24},{8,25},{9,... | collective-permute-start | bytes 2312 | tf_op jit(solution)/shard_map/ppermute | solution.py:29
  145.1 21.2 %collective-permute-start.9 = (bf16[192,12,128]{2,0,1:T(8,128)(2,1)}, bf16[192,12,128]{2,0,1:T(8,128)(2,1)S(1)}, u32[]{:S(2)}, u32[]{:S(2)}) collective-permute-start(bf16[192,12,128]{2,0,1:T(8,128)(2,1)} %copy.127), channel_id=1, source_target_pairs={{16,0},{17,1},{18,2},{19,3},{20,4},{21,5},{22,6},{23,7},{24,8},{25... | collective-permute-start | bytes 1769480 | tf_op jit(solution)/shard_map/ppermute | solution.py:29
  147.9 23.3 %collective-permute-start.10 = (bf16[192,12,128]{2,0,1:T(8,128)(2,1)}, bf16[192,12,128]{2,0,1:T(8,128)(2,1)S(1)}, u32[]{:S(2)}, u32[]{:S(2)}) collective-permute-start(bf16[192,12,128]{2,0,1:T(8,128)(2,1)} %copy.129), channel_id=1, source_target_pairs={{15,0},{16,1},{17,2},{18,3},{19,4},{20,5},{21,6},{22,7},{23,8},{24... | collective-permute-start | bytes 1769480 | tf_op jit(solution)/shard_map/ppermute | solution.py:29
  150.6 20.6 %copy-start.6 = (bf16[192,12,128]{2,0,1:T(8,128)(2,1)S(1)}, bf16[192,12,128]{2,0,1:T(8,128)(2,1)}, u32[]{:S(2)}) copy-start(bf16[192,12,128]{2,0,1:T(8,128)(2,1)} %copy.139) | copy-start | bytes 1769476
  150.6 24.2 %collective-permute-start.11 = (bf16[192,12,128]{2,0,1:T(8,128)(2,1)}, bf16[192,12,128]{2,0,1:T(8,128)(2,1)S(1)}, u32[]{:S(2)}, u32[]{:S(2)}) collective-permute-start(bf16[192,12,128]{2,0,1:T(8,128)(2,1)} %copy.131), channel_id=1, source_target_pairs={{1,0},{2,1},{3,2},{4,3},{5,4},{6,5},{7,6},{8,7},{9,8},{10,9},{11,1... | collective-permute-start | bytes 1769480 | tf_op jit(solution)/shard_map/ppermute | solution.py:29
  157.1 24.6 %collective-permute-start.12 = (bf16[192,12,128]{2,0,1:T(8,128)(2,1)}, bf16[192,12,128]{2,0,1:T(8,128)(2,1)S(1)}, u32[]{:S(2)}, u32[]{:S(2)}) collective-permute-start(bf16[192,12,128]{2,0,1:T(8,128)(2,1)} %copy.133), channel_id=1, source_target_pairs={{0,1},{1,2},{2,3},{3,4},{4,5},{5,6},{6,7},{7,8},{8,9},{9,10},{10,1... | collective-permute-start | bytes 1769480 | tf_op jit(solution)/shard_map/ppermute | solution.py:29
  159.3 23.7 %collective-permute-start.13 = (bf16[192,12,128]{2,0,1:T(8,128)(2,1)}, bf16[192,12,128]{2,0,1:T(8,128)(2,1)S(1)}, u32[]{:S(2)}, u32[]{:S(2)}) collective-permute-start(bf16[192,12,128]{2,0,1:T(8,128)(2,1)} %copy.135), channel_id=1, source_target_pairs={{0,15},{1,16},{2,17},{3,18},{4,19},{5,20},{6,21},{7,22},{8,23},{9,... | collective-permute-start | bytes 1769480 | tf_op jit(solution)/shard_map/ppermute | solution.py:29
  166.3 18.2 %collective-permute-start.14 = (bf16[192,12,128]{2,0,1:T(8,128)(2,1)}, bf16[192,12,128]{2,0,1:T(8,128)(2,1)S(1)}, u32[]{:S(2)}, u32[]{:S(2)}) collective-permute-start(bf16[192,12,128]{2,0,1:T(8,128)(2,1)} %copy.137), channel_id=1, source_target_pairs={{0,16},{1,17},{2,18},{3,19},{4,20},{5,21},{6,22},{7,23},{8,24},{9,... | collective-permute-start | bytes 1769480 | tf_op jit(solution)/shard_map/ppermute | solution.py:29
  171.2 22.6 %collective-permute-start.15 = (bf16[192,12,128]{2,0,1:T(8,128)(2,1)S(1)}, bf16[192,12,128]{2,0,1:T(8,128)(2,1)S(1)}, u32[]{:S(2)}, u32[]{:S(2)}) collective-permute-start(bf16[192,12,128]{2,0,1:T(8,128)(2,1)S(1)} %copy-done.6), channel_id=1, source_target_pairs={{0,17},{1,18},{2,19},{3,20},{4,21},{5,22},{6,23},{7,24},{8,25},{9,... | collective-permute-start | bytes 1769480 | tf_op jit(solution)/shard_map/ppermute | solution.py:29
  204.1 5.5 %collective-permute-start.21 = (f32[1,12,128]{2,0,1:T(1,128)S(1)}, f32[1,12,128]{2,0,1:T(1,128)S(1)}, u32[]{:S(2)}, u32[]{:S(2)}) collective-permute-start(f32[1,12,128]{2,0,1:T(1,128)S(1)} %get-tuple-element.23), channel_id=1, source_target_pairs={{16,0},{32,16},{48,32},{64,48},{80,64},{96,80},{112,96},{17,1},{33... | collective-permute-start | bytes 18440 | tf_op jit(solution)/shard_map/ppermute | solution.py:21
  206.0 4.9 %collective-permute-start.20 = (f32[1,12,128]{2,0,1:T(1,128)S(1)}, f32[1,12,128]{2,0,1:T(1,128)S(1)}, u32[]{:S(2)}, u32[]{:S(2)}) collective-permute-start(f32[1,12,128]{2,0,1:T(1,128)S(1)} %get-tuple-element.22), channel_id=1, source_target_pairs={{0,16},{16,32},{32,48},{48,64},{64,80},{80,96},{96,112},{1,17},{17... | collective-permute-start | bytes 18440 | tf_op jit(solution)/shard_map/ppermute | solution.py:20
  211.3 16.4 %copy-start.7 = (f32[256,128]{0,1:T(8,128)S(1)}, f32[256,128]{0,1:T(8,128)}, u32[]{:S(2)}) copy-start(f32[256,128]{0,1:T(8,128)} %copy.153) | copy-start | bytes 393220
  211.3 16.4 %copy-start.8 = (f32[256,128]{0,1:T(8,128)S(1)}, f32[256,128]{0,1:T(8,128)}, u32[]{:S(2)}) copy-start(f32[256,128]{0,1:T(8,128)} %copy.150) | copy-start | bytes 393220
  211.3 16.3 %copy-start.9 = (f32[256,128]{0,1:T(8,128)S(1)}, f32[256,128]{0,1:T(8,128)}, u32[]{:S(2)}) copy-start(f32[256,128]{0,1:T(8,128)} %copy.147) | copy-start | bytes 393220
  211.5 10.4 %collective-permute-start.23 = (f32[258,12,1]{0,2,1:T(1,128)S(1)}, f32[258,12,1]{0,2,1:T(1,128)S(1)}, u32[]{:S(2)}, u32[]{:S(2)}) collective-permute-start(f32[258,12,1]{0,2,1:T(1,128)S(1)} %get-tuple-element.21), channel_id=1, source_target_pairs={{1,0},{2,1},{3,2},{4,3},{5,4},{6,5},{7,6},{8,7},{9,8},{10,9},{11,1... | collective-permute-start | bytes 37160 | tf_op jit(solution)/shard_map/ppermute | solution.py:21
  219.9 7.8 %collective-permute-start.22 = (f32[258,12,1]{0,2,1:T(1,128)S(1)}, f32[258,12,1]{0,2,1:T(1,128)S(1)}, u32[]{:S(2)}, u32[]{:S(2)}) collective-permute-start(f32[258,12,1]{0,2,1:T(1,128)S(1)} %get-tuple-element.20), channel_id=1, source_target_pairs={{0,1},{1,2},{2,3},{3,4},{4,5},{5,6},{6,7},{7,8},{8,9},{9,10},{10,1... | collective-permute-start | bytes 37160 | tf_op jit(solution)/shard_map/ppermute | solution.py:20
  (17 other events, 95.3 us)
where the time goes:
time: 235 us; the launch traced here: 234 us
  local copies, waits for them, and re-layouts  83.5 us (36%)
  starting transfers between devices  82.1 us (35%)
  matrix products  31.2 us (13%)
  waiting for transfers between devices  23.1 us (10%)
  other arithmetic  12.4 us (5%)
    ppermute x16, starting transfers between devices, from_behind(): lax.ppermute(value, axis, [(source, source + steps) for source in range(i...  54 us
    gather x1, local copies, waits for them, and re-layouts, per_device(): tile_pick = weight_tiles[tile_index]  23.9 us
    ppermute x4, starting transfers between devices, extended(): after = lax.ppermute(initial, axis, down)  19.6 us
    dot_general x1, matrix products, per_device(): jnp.einsum('snk,sck->scn', tile_pick, block_pick, preferred_element_type=...  18.4 us
    ppermute x16, waiting for transfers between devices, from_behind(): lax.ppermute(value, axis, [(source, source + steps) for source in range(i...  16.3 us
    squeeze x9, local copies, waits for them, and re-layouts, per_device(): outgoing[move_x + 1, move_y + 1]  14.8 us
    unnamed x65, local copies, waits for them, and re-layouts  12.6 us
    reshape x1, local copies, waits for them, and re-layouts, per_device(): outgoing.astype(jnp.bfloat16)  10.4 us
  transfers between devices with their start and end apart: 24, of which 7 were waited for; matrix products, arithmetic and copies ran while one was open for 10% of the time, Pallas kernels for 0%

commit v1 on v0

v1 whole, which is shorter than its diff:
```python
import functools

import jax
import jax.numpy as jnp
from jax import lax
from jax.experimental import pallas as pl
from jax.experimental.pallas import tpu as pltpu
from jax.sharding import PartitionSpec as P

time_step = 0.2
shape_factor = 0.95
interaction = 0.01
shear_modulus = 1.0
fiber_number = 2.0

MESH = pl.DeviceIdType.MESH
CHUNK = 48
HALO_ROWS = 14
MIB = 1 << 20


def step_of(k):
    m = k // 2
    dx = jnp.where(k < 6, jnp.where(m == 2, 0, 2 * m - 1), 2 * (k - 6) - 1)
    dy = jnp.where(k < 6, 1 - 2 * (k % 2), 0)
    return dx, dy


def exists(x, y, nx, ny):
    return (x >= 0) & (x < nx) & (y >= 0) & (y < ny)


def neighbours_of(x, y, nx, ny):
    spread_x = 3 - (x == 0).astype(jnp.int32) - (x == nx - 1).astype(jnp.int32)
    spread_y = 3 - (y == 0).astype(jnp.int32) - (y == ny - 1).astype(jnp.int32)
    return spread_x * spread_y - 1


def chunks_of(x, y, nx, ny, caps):
    n = neighbours_of(x, y, nx, ny)
    inner, edge, corner = caps
    return jnp.where(n >= 8, inner, jnp.where(n >= 5, edge, corner))


def exchange_kernel(
    nx,
    ny,
    caps,
    picks,
    labels,
    old,
    vel,
    weights,
    remapped,
    halo_y,
    halo_x,
    tiles,
    outgoing,
    incoming,
    incoming_labels,
    turn,
    edge_y,
    edge_x,
    load_sem,
    label_sems,
    send_sems,
    recv_sems,
    edge_sems,
):
    gx, gy = lax.axis_index("gx"), lax.axis_index("gy")
    parts = load_sem.shape[0]
    depth = tiles.shape[0] // parts
    cap = outgoing.shape[1]
    rows = remapped.shape[1]
    state_count = remapped.shape[0]

    for part in range(parts):
        span = pl.ds(part * depth, depth)
        pltpu.make_async_copy(weights.at[span], tiles.at[span], load_sem.at[part]).start()

    barrier = pltpu.get_barrier_semaphore()
    for k in range(8):
        dx, dy = step_of(k)

        @pl.when(exists(gx + dx, gy + dy, nx, ny))
        def _():
            pl.semaphore_signal(
                barrier, inc=1, device_id=(gx + dx, gy + dy), device_id_type=MESH
            )

    pl.semaphore_wait(barrier, neighbours_of(gx, gy, nx, ny))

    def label_copy(k):
        dx, dy = step_of(k)
        return pltpu.make_async_remote_copy(
            src_ref=labels.at[k],
            dst_ref=incoming_labels.at[k],
            send_sem=label_sems.at[0, k],
            recv_sem=label_sems.at[1, k],
            device_id=(gx + dx, gy + dy),
            device_id_type=MESH,
        )

    def chunk_copy(k, j):
        dx, dy = step_of(k)
        span = pl.ds(j * CHUNK, CHUNK)
        return pltpu.make_async_remote_copy(
            src_ref=outgoing.at[k, span],
            dst_ref=incoming.at[k, span],
            send_sem=send_sems.at[k, j],
            recv_sem=recv_sems.at[k, j],
            device_id=(gx + dx, gy + dy),
            device_id_type=MESH,
        )

    def goes_out(k):
        dx, dy = step_of(k)
        return exists(gx + dx, gy + dy, nx, ny)

    def comes_in(k):
        dx, dy = step_of(k)
        return exists(gx - dx, gy - dy, nx, ny)

    def each_channel(body, predicate):
        def step(k, carry):
            @pl.when(predicate(k))
            def _():
                body(k)

            return carry

        lax.fori_loop(0, 8, step, 0)

    each_channel(lambda k: label_copy(k).start(), goes_out)

    for part in range(parts):
        span = pl.ds(part * depth, depth)
        pltpu.make_async_copy(weights.at[span], tiles.at[span], load_sem.at[part]).wait()

    def compute_chunk(k, j):
        for i in range(CHUNK):
            pick = picks[k * cap + j * CHUNK + i]
            piece = lax.dot_general(
                old[pick & 127],
                tiles[pick >> 7],
                (((1,), (1,)), ((), ())),
                preferred_element_type=jnp.float32,
            )
            turn[pl.ds(16 * i, 16), :] = piece
        for group in range(CHUNK // 16):
            for c in range(state_count):
                turned = turn[pl.ds(256 * group + c, 16, stride=16), :]
                outgoing[
                    k,
                    pl.ds(pl.multiple_of(j * CHUNK + 16 * group, 16), 16),
                    pl.ds(c * 128, 128),
                ] = turned.astype(jnp.bfloat16)

    count = chunks_of(gx, gy, nx, ny, caps)

    def channel(k):
        def chunk(j, carry):
            compute_chunk(k, j)
            chunk_copy(k, j).start()
            return carry

        lax.fori_loop(0, count, chunk, 0)

    each_channel(channel, goes_out)

    def own_chunk(j, carry):
        compute_chunk(8, j)
        return carry

    lax.fori_loop(0, cap // CHUNK, own_chunk, 0)

    row_ids = lax.broadcasted_iota(jnp.int32, (rows, 128), 0)

    def add(label_row, values, first):
        width = values.shape[0]
        selector = jnp.where(row_ids == label_row, 1.0, 0.0).astype(jnp.bfloat16)[:, :width]
        for c in range(0, state_count, 2):
            summed = jnp.dot(
                selector,
                values[:, c * 128 : (c + 2) * 128],
                preferred_element_type=jnp.float32,
            )
            if first:
                remapped[c] = summed[:, :128]
                remapped[c + 1] = summed[:, 128:]
            else:
                remapped[c] += summed[:, :128]
                remapped[c + 1] += summed[:, 128:]

    add(labels[8, 0:1, :], outgoing[8, 0 : 2 * CHUNK], True)
    add(labels[8, 1:2, :], outgoing[8, 2 * CHUNK : 4 * CHUNK], False)

    def accept(k):
        dx, dy = step_of(k)
        arriving = chunks_of(gx - dx, gy - dy, nx, ny, caps)
        label_copy(k).wait_recv()
        chunk_copy(k, 0).wait_recv()
        chunk_copy(k, 1).wait_recv()
        add(incoming_labels[k, 0:1, :], incoming[k, 0 : 2 * CHUNK], False)
        for j in (2, 3):

            @pl.when(arriving > j)
            def _():
                chunk_copy(k, j).wait_recv()
                add(
                    incoming_labels[k, j : j + 1, :],
                    incoming[k, j * CHUNK : (j + 1) * CHUNK],
                    False,
                )

    each_channel(accept, comes_in)

    lanes = lax.broadcasted_iota(jnp.int32, (32, 128), 1)
    for side, lane in ((0, 127), (1, 0)):
        packed = jnp.zeros((32, 128), jnp.float32)
        for b in range(rows // 32):
            for c in range(HALO_ROWS):
                ref = remapped.at[c] if c < state_count else vel.at[c - state_count]
                to = 16 * b + c
                moved = pltpu.roll(ref[pl.ds(32 * b, 32), :], (to - lane) % 128, 1)
                packed = jnp.where(lanes == to, moved, packed)
        edge_y[side] = packed
    for side, row in ((0, rows - 1), (1, 0)):
        for c in range(HALO_ROWS):
            ref = remapped.at[c] if c < state_count else vel.at[c - state_count]
            edge_x[side, c : c + 1, :] = ref[row : row + 1, :]
    sides = (
        (edge_y, halo_y, 0, 0, 1),
        (edge_y, halo_y, 1, 0, -1),
        (edge_x, halo_x, 0, 1, 0),
        (edge_x, halo_x, 1, -1, 0),
    )

    def side_copy(index):
        edge, _, side, dx, dy = sides[index]
        return pltpu.make_async_remote_copy(
            src_ref=edge.at[side],
            dst_ref=edge.at[side + 2],
            send_sem=edge_sems.at[0, index],
            recv_sem=edge_sems.at[1, index],
            device_id=(gx + dx, gy + dy),
            device_id_type=MESH,
        )

    for index, (_, _, _, dx, dy) in enumerate(sides):

        @pl.when(exists(gx + dx, gy + dy, nx, ny))
        def _():
            side_copy(index).start()

    for index, (edge, halo, side, dx, dy) in enumerate(sides):
        there = exists(gx - dx, gy - dy, nx, ny)

        @pl.when(there)
        def _():
            side_copy(index).wait_recv()
            halo[side] = edge[side + 2]

        @pl.when(jnp.logical_not(there))
        def _():
            halo[side] = jnp.zeros(halo.shape[1:], jnp.float32)

    for index, (_, _, _, dx, dy) in enumerate(sides):

        @pl.when(exists(gx + dx, gy + dy, nx, ny))
        def _():
            side_copy(index).wait_send()

    def finish(k):
        label_copy(k).wait_send()

        def chunk(j, carry):
            chunk_copy(k, j).wait_send()
            return carry

        lax.fori_loop(0, count, chunk, 0)

    each_channel(finish, goes_out)


def exchange(nx, ny, caps, collective_id, picks, labels, old, velocity, weights):
    state_count, rows = old.shape[1] // 16 * 12, velocity.shape[1]
    cap = labels.shape[2] // 128 * 192
    f32, vmem = jnp.float32, pltpu.VMEM
    in_vmem = pl.BlockSpec(memory_space=vmem)
    dma = pltpu.SemaphoreType.DMA
    return pl.pallas_call(
        functools.partial(exchange_kernel, nx, ny, caps),
        out_shape=(
            jax.ShapeDtypeStruct((state_count, rows, 128), f32),
            jax.ShapeDtypeStruct((2, 32, 128), f32),
            jax.ShapeDtypeStruct((2, 16, 128), f32),
        ),
        in_specs=[
            pl.BlockSpec(memory_space=pltpu.SMEM),
            in_vmem,
            in_vmem,
            in_vmem,
            pl.BlockSpec(memory_space=pl.ANY),
        ],
        out_specs=(in_vmem,) * 3,
        scratch_shapes=[
            vmem(weights.shape, jnp.bfloat16),
            vmem((9, cap, state_count * 128), jnp.bfloat16),
            vmem((8, cap, state_count * 128), jnp.bfloat16),
            vmem((8, 8, 128), jnp.int32),
            vmem((16 * CHUNK, 128), f32),
            vmem((4, 32, 128), f32),
            vmem((4, 16, 128), f32),
            dma((4,)),
            dma((2, 8)),
            dma((8, cap // CHUNK)),
            dma((8, cap // CHUNK)),
            dma((2, 4)),
        ],
        compiler_params=pltpu.CompilerParams(
            collective_id=collective_id, has_side_effects=True, vmem_limit_bytes=48 * MIB
        ),
        cost_estimate=pl.CostEstimate(
            flops=2 * picks.shape[0] * 128 * 128 * 16,
            bytes_accessed=weights.size * 2,
            transcendentals=0,
        ),
    )(picks, labels, old, velocity, weights)


def step_kernel(state, halo_y, halo_x, vel, out):
    b = pl.program_id(0)
    blocks = pl.num_programs(0)
    states, rows, depth = state.shape[0], state.shape[1], 32
    base = pl.multiple_of(b * depth, depth)
    lane = lax.broadcasted_iota(jnp.int32, (depth, 128), 1)
    row = lax.broadcasted_iota(jnp.int32, (depth, 128), 0)
    left_pack = pltpu.roll(halo_y[0], lax.rem(128 - 16 * b, 128), 1)
    right_pack = pltpu.roll(halo_y[1], lax.rem(128 + 127 - 16 * b, 128), 1)

    def around(ref, index, c):
        mid = ref[index, pl.ds(base, depth), :]
        above = jnp.where(b == 0, halo_x[0, c : c + 1, :], ref[index, pl.ds(jnp.maximum(base - 1, 0), 1), :])
        below = jnp.where(
            b == blocks - 1,
            halo_x[1, c : c + 1, :],
            ref[index, pl.ds(jnp.minimum(base + depth, rows - 1), 1), :],
        )
        before_x = jnp.where(row == 0, above, pltpu.roll(mid, 1, 0))
        after_x = jnp.where(row == depth - 1, below, pltpu.roll(mid, depth - 1, 0))
        shift = (128 - c) % 128
        before_y = jnp.where(lane == 0, pltpu.roll(left_pack, shift, 1), pltpu.roll(mid, 1, 1))
        after_y = jnp.where(lane == 127, pltpu.roll(right_pack, shift, 1), pltpu.roll(mid, 127, 1))
        return mid, before_x, after_x, before_y, after_y

    u_x, ux_bx, ux_ax, ux_by, ux_ay = around(vel, 0, states)
    u_y, uy_bx, uy_ax, uy_by, uy_ay = around(vel, 1, states + 1)
    d_xx = 0.5 * (ux_ax - ux_bx)
    l_xy = 0.5 * (ux_ay - ux_by)
    l_yx = 0.5 * (uy_ax - uy_bx)
    d_yy = 0.5 * (uy_ay - uy_by)
    d_zz = -(d_xx + d_yy)
    d_xy = 0.5 * (l_xy + l_yx)
    spin = 0.5 * (l_xy - l_yx)
    plus_x, minus_x = jnp.maximum(u_x, 0.0), jnp.minimum(u_x, 0.0)
    plus_y, minus_y = jnp.maximum(u_y, 0.0), jnp.minimum(u_y, 0.0)
    shear = (2.0 * interaction) * jnp.sqrt(
        2.0 * (d_xx * d_xx + d_yy * d_yy + d_zz * d_zz + 2.0 * (d_xy * d_xy)) + 1.0
    )
    a_xx, a_yy, a_zz, a_xy, a_xz, a_yz = (state[c, pl.ds(base, depth), :] for c in range(6))
    contraction = d_xx * a_xx + d_yy * a_yy + d_zz * a_zz + 2.0 * (d_xy * a_xy)
    fade = shape_factor * 2.0 * contraction + 3.0 * shear
    stress = 2.0 * shear_modulus
    pull = fiber_number * contraction
    sources = (
        2.0 * (spin * a_xy) + shape_factor * 2.0 * (d_xx * a_xx + d_xy * a_xy) - fade * a_xx + shear,
        -2.0 * (spin * a_xy) + shape_factor * 2.0 * (d_xy * a_xy + d_yy * a_yy) - fade * a_yy + shear,
        shape_factor * 2.0 * (d_zz * a_zz) - fade * a_zz + shear,
        spin * (a_yy - a_xx)
        + shape_factor * (d_xx * a_xy + d_xy * a_yy + a_xx * d_xy + a_xy * d_yy)
        - fade * a_xy,
        spin * a_yz + shape_factor * (d_xx * a_xz + d_xy * a_yz + a_xz * d_zz) - fade * a_xz,
        -spin * a_xz + shape_factor * (d_xy * a_xz + d_yy * a_yz + a_yz * d_zz) - fade * a_yz,
        d_xx,
        d_yy,
        d_xy,
        stress * (d_xx + pull * a_xx),
        stress * (d_yy + pull * a_yy),
        stress * (d_xy + pull * a_xy),
    )
    for c, source in enumerate(sources):
        mid, before_x, after_x, before_y, after_y = around(state, c, c)
        upwind = (
            plus_x * (mid - before_x)
            + minus_x * (after_x - mid)
            + plus_y * (mid - before_y)
            + minus_y * (after_y - mid)
        )
        out[c] = mid + time_step * (source - upwind)


def advance(state, halo_y, halo_x, velocity):
    in_vmem = pl.BlockSpec(memory_space=pltpu.VMEM)
    states, rows, width = state.shape
    return pl.pallas_call(
        step_kernel,
        grid=(rows // 32,),
        out_shape=jax.ShapeDtypeStruct(state.shape, jnp.float32),
        in_specs=[in_vmem] * 4,
        out_specs=pl.BlockSpec((states, 32, width), lambda b: (0, b, 0)),
        compiler_params=pltpu.CompilerParams(vmem_limit_bytes=24 * MIB),
    )(state, halo_y, halo_x, velocity)


def plan(source_block, tile_index, dest_device, dest_block, send_count, ny):
    slots = source_block.shape[0]
    cap = slots // 4
    live = jnp.arange(slots) < send_count[0]
    sx = dest_device // ny - lax.axis_index("gx")
    sy = dest_device % ny - lax.axis_index("gy")
    m = jnp.where(sx == 0, 2, (sx + 1) // 2)
    channel = jnp.where(sy == 0, jnp.where(sx == 0, 8, 6 + (sx + 1) // 2), 2 * m + (sy < 0))
    channel = jnp.where(live, channel, 9)
    matches = channel[None, :] == jnp.arange(9)[:, None]
    earlier = jnp.arange(slots)[:, None] < jnp.arange(slots)[None, :]
    position = jnp.dot(
        matches.astype(jnp.bfloat16),
        earlier.astype(jnp.bfloat16),
        preferred_element_type=jnp.float32,
    )
    position = jnp.sum(jnp.where(matches, position, 0.0), axis=0).astype(jnp.int32)
    target = jnp.where(live, channel * cap + position, -1)
    value = (tile_index * 128 + source_block) * 512 + dest_block + 1
    value = jnp.sum(
        jnp.where(target[None, :] == jnp.arange(9 * cap)[:, None], value[None, :], 0), axis=1
    )
    rows = (value % 512 - 1).reshape(9, cap)
    half, quarter = cap // 2, cap // 4
    pieces = (rows[:, :half], rows[:, half:], rows[:, half : half + quarter], rows[:, half + quarter :])
    pieces = [jnp.pad(p, ((0, 0), (0, 128 - p.shape[1]))) for p in pieces]
    labels = jnp.pad(jnp.stack(pieces, axis=1), ((0, 0), (0, 4), (0, 0)))
    return value // 512, labels


def per_device(
    nx,
    ny,
    old_states,
    weight_tiles,
    source_block,
    tile_index,
    dest_device,
    dest_block,
    send_count,
    velocity,
):
    picks, labels = plan(source_block, tile_index, dest_device, dest_block, send_count, ny)
    old = jnp.pad(old_states, ((0, 0), (0, 4), (0, 0)))
    state, halo_y, halo_x = exchange(
        nx, ny, (4, 4, 4), 0, picks, labels, old, velocity, weight_tiles
    )
    return jnp.transpose(advance(state, halo_y, halo_x, velocity), (1, 0, 2))


def solution(mesh):
    in_specs = (
        P(("gx", "gy"), None, None),
        P(("gx", "gy"), None, None),
        P(("gx", "gy")),
        P(("gx", "gy")),
        P(("gx", "gy")),
        P(("gx", "gy")),
        P(("gx", "gy")),
        P(None, "gx", "gy"),
    )
    out_specs = P("gx", None, "gy")
    return jax.shard_map(
        functools.partial(per_device, mesh.shape["gx"], mesh.shape["gy"]),
        mesh=mesh,
        in_specs=in_specs,
        out_specs=out_specs,
        check_vma=False,
    )
```

time: 235 us -> 73.8 us (0.31)
  the two profiles are of different devices: /device:TPU:10 before, /device:TPU:14 now
where the time goes in v1:
time: 73.8 us; the launch traced here: 73.6 us
  Pallas kernels  67.2 us (91%)
  other arithmetic  2.81 us (4%)
  local copies, waits for them, and re-layouts  2.59 us (4%)
  between operations  0.74 us (1%)
    pallas_call x1, Pallas kernels, exchange(): pl.pallas_call(functools.partial(exchange_kernel, nx, ny, caps), out_shap...  62.6 us
    pallas_call x1, Pallas kernels, advance(): pl.pallas_call(step_kernel, grid=(rows // 32,), out_shape=jax.ShapeDtypeS...  4.53 us
    unnamed x3, local copies, waits for them, and re-layouts  2.22 us

profile of v1, /device:TPU:14, one launch (start us, length us, event | category | flops | bytes accessed | tf_op | source)
XLA Modules:
  0.0 73.6 jit_solution(9025953462506778066)
XLA Ops:
  0.7 0.7 select_select_fusion
  1.4 0.2 fusion.2
  1.6 0.8 %add_add_fusion = (s32[768]{0:T(1024)S(1)}, s32[768]{0:T(1024)S(1)}) fusion(s32[768]{0:T(1024)} %param.13, s32[768]{0:T(1024)} %param.10, s32[768]{0:T(1024)} %param.11, f32[768]{0:T(1024)S(1)} %fusion.2, s32[]{:T(128)} %bitcast.9, s32[]{:T(128)S(6)} %axis_index.25, s32[768]{0:T(1024)} %param.12, s32[]{:T(128)S(6)} %axis_index.22), kind=kLoop, calls=%fused_computation.37 | loop fusion | flops 44544 | bytes 21516 | tf_op jit(solution)/shard_map/add | solution.py:434
  2.4 0.6 select_reduce_fusion
  3.0 0.1 reduce_sum.22
  3.1 0.1 slice.18
  3.2 0.7 fusion.7
  3.9 0.1 fusion.15
  4.0 1.3 %copy.16 = bf16[128,12,128]{2,1,0:T(8,128)(2,1)S(1)} copy(bf16[128,12,128]{2,0,1:T(8,128)(2,1)} %param.8) | data formatting | bytes 786432 | tf_op args[0]
  5.3 0.1 pad.27.old
  5.4 0.0 copy-start
  5.4 0.9 %copy-done = f32[2,256,128]{2,1,0:T(8,128)S(1)} copy-done((f32[2,256,128]{2,1,0:T(8,128)S(1)}, f32[2,256,128]{2,1,0:T(8,128)}, u32[]{:S(2)}) %copy-start) | copy-done | bytes 262168
  6.4 62.6 %shard_map.82 = (f32[12,256,128]{2,1,0:T(8,128)S(1)}, f32[2,32,128]{2,1,0:T(8,128)S(1)}, f32[2,16,128]{2,1,0:T(8,128)S(1)}) custom-call(s32[1728]{0:T(1024)S(1)} %add_select_fusion.1.picks, s32[9,8,128]{2,1,0:T(8,128)S(1)} %pad.26.labels, bf16[128,16,128]{2,1,0:T(8,128)(2,1)S(1)} %pad.27.old, f32[2,256,128]{2,1,0:T(8,128)S(1)} %copy-done, ...), custom_call_target="tpu_custom_call" | custom-call | flops 905969664 | bytes 12582912 | tf_op jit(solution)/shard_map/pallas_call | solution.py:292
  69.0 4.5 %shard_map.83 = f32[12,256,128]{2,1,0:T(8,128)} custom-call(f32[12,256,128]{2,1,0:T(8,128)S(1)} %get-tuple-element.8.state, f32[2,32,128]{2,1,0:T(8,128)S(1)} %get-tuple-element.9.halo_y, f32[2,16,128]{2,1,0:T(8,128)S(1)} %get-tuple-element.10.halo_x, f32[2,256,128]{2,1,0:T(8,128)S(1)} %copy-done), custom_call_target="tpu_custom_call" | custom-call | tf_op jit(solution)/shard_map/pallas_call | solution.py:406
  (11 shorter events, 0.1 us)
Async XLA Ops:
  5.4 1.0 %copy-start = (f32[2,256,128]{2,1,0:T(8,128)S(1)}, f32[2,256,128]{2,1,0:T(8,128)}, u32[]{:S(2)}) copy-start(f32[2,256,128]{2,1,0:T(8,128)} %vel.3) | copy-start | bytes 786436

commit v2 on v1

--- a/solution.py
+++ b/solution.py
@@ -16,6 +16,8 @@
 MESH = pl.DeviceIdType.MESH
 CHUNK = 48
 HALO_ROWS = 14
+USUAL = (2, 3, 4)
+FULL = (4, 4, 4)
 MIB = 1 << 20
 
 
@@ -40,6 +42,15 @@
     n = neighbours_of(x, y, nx, ny)
     inner, edge, corner = caps
     return jnp.where(n >= 8, inner, jnp.where(n >= 5, edge, corner))
+
+
+def mirrored(x, y, nx, ny, t):
+    bits_x = nx.bit_length() - 1
+    for step in range(bits_x):
+        x = jnp.where(t == step, x + (1 - 2 * (x // 2**step % 2)) * 2**step, x)
+    for step in range(ny.bit_length() - 1):
+        y = jnp.where(t == bits_x + step, y + (1 - 2 * (y // 2**step % 2)) * 2**step, y)
+    return x, y
 
 
 def exchange_kernel(
@@ -48,12 +59,14 @@
     caps,
     picks,
     labels,
+    over,
     old,
     vel,
     weights,
     remapped,
     halo_y,
     halo_x,
+    any_over,
     tiles,
     outgoing,
     incoming,
@@ -61,11 +74,14 @@
     turn,
     edge_y,
     edge_x,
+    flags,
+    flags_in,
     load_sem,
     label_sems,
     send_sems,
     recv_sems,
     edge_sems,
+    flag_sems,
 ):
     gx, gy = lax.axis_index("gx"), lax.axis_index("gy")
     parts = load_sem.shape[0]
@@ -88,7 +104,33 @@
                 barrier, inc=1, device_id=(gx + dx, gy + dy), device_id_type=MESH
             )
 
-    pl.semaphore_wait(barrier, neighbours_of(gx, gy, nx, ny))
+    swaps = flags_in.shape[0]
+    for t in range(swaps):
+        pl.semaphore_signal(
+            barrier, inc=1, device_id=mirrored(gx, gy, nx, ny, t), device_id_type=MESH
+        )
+    pl.semaphore_wait(barrier, neighbours_of(gx, gy, nx, ny) + swaps)
+
+    def flag_copy(t):
+        return pltpu.make_async_remote_copy(
+            src_ref=flags.at[t],
+            dst_ref=flags_in.at[t],
+            send_sem=flag_sems.at[0, t],
+            recv_sem=flag_sems.at[1, t],
+            device_id=mirrored(gx, gy, nx, ny, t),
+            device_id_type=MESH,
+        )
+
+    flags[0] = over[...]
+    flag_copy(0).start()
+
+    def pass_flag(t):
+        flag_copy(t).wait_recv()
+        flags[t + 1] = jnp.maximum(flags[t], flags_in[t])
+
+        @pl.when(t + 1 < swaps)
+        def _():
+            flag_copy(t + 1).start()
 
     def label_copy(k):
         dx, dy = step_of(k)
@@ -166,7 +208,18 @@
 
         lax.fori_loop(0, count, chunk, 0)
 
-    each_channel(channel, goes_out)
+    def channel_and_flag(k, carry):
+        @pl.when(goes_out(k))
+        def _():
+            channel(k)
+
+        @pl.when(k < swaps)
+        def _():
+            pass_flag(k)
+
+        return carry
+
+    lax.fori_loop(0, 8, channel_and_flag, 0)
 
     def own_chunk(j, carry):
         compute_chunk(8, j)
@@ -281,10 +334,14 @@
         lax.fori_loop(0, count, chunk, 0)
 
     each_channel(finish, goes_out)
-
-
-def exchange(nx, ny, caps, collective_id, picks, labels, old, velocity, weights):
-    state_count, rows = old.shape[1] // 16 * 12, velocity.shape[1]
+    for t in range(swaps):
+        flag_copy(t).wait_send()
+    any_over[...] = flags[swaps]
+
+
+def exchange(nx, ny, caps, collective_id, picks, labels, over, old, velocity, weights):
+    swaps = nx.bit_length() + ny.bit_length() - 2
+    state_count, rows = HALO_ROWS - 2, velocity.shape[1]
     cap = labels.shape[2] // 128 * 192
     f32, vmem = jnp.float32, pltpu.VMEM
     in_vmem = pl.BlockSpec(memory_space=vmem)
@@ -295,15 +352,17 @@
             jax.ShapeDtypeStruct((state_count, rows, 128), f32),
             jax.ShapeDtypeStruct((2, 32, 128), f32),
             jax.ShapeDtypeStruct((2, 16, 128), f32),
+            jax.ShapeDtypeStruct((8, 128), jnp.int32),
         ),
         in_specs=[
             pl.BlockSpec(memory_space=pltpu.SMEM),
             in_vmem,
             in_vmem,
             in_vmem,
+            in_vmem,
             pl.BlockSpec(memory_space=pl.ANY),
         ],
-        out_specs=(in_vmem,) * 3,
+        out_specs=(in_vmem,) * 4,
         scratch_shapes=[
             vmem(weights.shape, jnp.bfloat16),
             vmem((9, cap, state_count * 128), jnp.bfloat16),
@@ -312,11 +371,14 @@
             vmem((16 * CHUNK, 128), f32),
             vmem((4, 32, 128), f32),
             vmem((4, 16, 128), f32),
+            vmem((swaps + 1, 8, 128), jnp.int32),
+            vmem((swaps, 8, 128), jnp.int32),
             dma((4,)),
             dma((2, 8)),
             dma((8, cap // CHUNK)),
             dma((8, cap // CHUNK)),
             dma((2, 4)),
+            dma((2, swaps)),
         ],
         compiler_params=pltpu.CompilerParams(
             collective_id=collective_id, has_side_effects=True, vmem_limit_bytes=48 * MIB
@@ -326,7 +388,7 @@
             bytes_accessed=weights.size * 2,
             transcendentals=0,
         ),
-    )(picks, labels, old, velocity, weights)
+    )(picks, labels, over, old, velocity, weights)
 
 
 def step_kernel(state, halo_y, halo_x, vel, out):
@@ -413,7 +475,7 @@
     )(state, halo_y, halo_x, velocity)
 
 
-def plan(source_block, tile_index, dest_device, dest_block, send_count, ny):
+def plan(source_block, tile_index, dest_device, dest_block, send_count, caps, nx, ny):
     slots = source_block.shape[0]
     cap = slots // 4
     live = jnp.arange(slots) < send_count[0]
@@ -440,7 +502,10 @@
     pieces = (rows[:, :half], rows[:, half:], rows[:, half : half + quarter], rows[:, half + quarter :])
     pieces = [jnp.pad(p, ((0, 0), (0, 128 - p.shape[1]))) for p in pieces]
     labels = jnp.pad(jnp.stack(pieces, axis=1), ((0, 0), (0, 4), (0, 0)))
-    return value // 512, labels
+    counts = jnp.sum(matches.astype(jnp.int32), axis=1)[:8]
+    allowed = chunks_of(lax.axis_index("gx"), lax.axis_index("gy"), nx, ny, caps) * CHUNK
+    over = jnp.broadcast_to((jnp.max(counts) > allowed).astype(jnp.int32), (8, 128))
+    return value // 512, labels, over
 
 
 def per_device(
@@ -455,12 +520,23 @@
     send_count,
     velocity,
 ):
-    picks, labels = plan(source_block, tile_index, dest_device, dest_block, send_count, ny)
+    picks, labels, over = plan(
+        source_block, tile_index, dest_device, dest_block, send_count, USUAL, nx, ny
+    )
     old = jnp.pad(old_states, ((0, 0), (0, 4), (0, 0)))
-    state, halo_y, halo_x = exchange(
-        nx, ny, (4, 4, 4), 0, picks, labels, old, velocity, weight_tiles
-    )
-    return jnp.transpose(advance(state, halo_y, halo_x, velocity), (1, 0, 2))
+    *edges, any_over = exchange(
+        nx, ny, USUAL, 0, picks, labels, over, old, velocity, weight_tiles
+    )
+
+    def again(*_):
+        *edges, _ = exchange(nx, ny, FULL, 1, picks, labels, over, old, velocity, weight_tiles)
+        return advance(*edges, velocity)
+
+    def enough(*edges):
+        return advance(*edges, velocity)
+
+    states = lax.cond(any_over[0, 0] > 0, again, enough, *edges)
+    return jnp.transpose(states, (1, 0, 2))
 
 
 def solution(mesh):

time: 73.8 us -> 69.5 us (0.942)
  the two profiles are of different devices: /device:TPU:14 before, /device:TPU:24 now
where the time goes in v2:
time: 69.5 us; the launch traced here: 69.2 us
  Pallas kernels  59.8 us (86%)
  other arithmetic  3.65 us (5%)
  local copies, waits for them, and re-layouts  3.3 us (5%)
  between operations  2.16 us (3%)
    pallas_call x1, Pallas kernels, exchange(): pl.pallas_call(functools.partial(exchange_kernel, nx, ny, caps), out_shap...  56.9 us
    pallas_call x1, Pallas kernels, advance(): pl.pallas_call(step_kernel, grid=(rows // 32,), out_shape=jax.ShapeDtypeS...  2.91 us
    unnamed x5, local copies, waits for them, and re-layouts  2.41 us

profile of v2, /device:TPU:24, one launch (start us, length us, event | category | flops | bytes accessed | tf_op | source)
XLA Modules:
  0.0 69.2 jit_solution(16388060080570460640)
XLA Ops:
  0.0 0.0 copy-start
  0.7 0.7 %select_select_fusion = s32[768]{0:T(1024)S(1)} fusion(s32[768]{0:T(1024)} %param.14, s32[]{:T(128)S(6)} %axis_index.33, s32[]{:T(128)S(6)} %axis_index.14, s32[]{:T(128)} %bitcast.9), kind=kLoop, calls=%fused_computation.40 | loop fusion | flops 37632 | bytes 6156 | tf_op jit(solution)/shard_map/jit(_where)/select_n | solution.py:486
  1.4 0.1 convert_reduce_fusion
  1.5 0.7 %slice_reduce_fusion = s32[]{:T(128)} fusion(s32[9]{0:T(128)S(1)} %convert_reduce_fusion), kind=kLoop, calls=%fused_computation.47 | loop fusion | flops 7 | bytes 36 | tf_op jit(solution)/shard_map/reduce_max | solution.py:507
  2.9 0.2 fusion.2
  3.2 0.8 %add_add_fusion = (s32[768]{0:T(1024)S(1)}, s32[768]{0:T(1024)S(1)}) fusion(s32[768]{0:T(1024)} %param.15, s32[768]{0:T(1024)} %param.12, s32[768]{0:T(1024)} %param.13, f32[768]{0:T(1024)S(1)} %fusion.2, s32[]{:T(128)} %bitcast.10, s32[]{:T(128)S(6)} %axis_index.33, s32[768]{0:T(1024)} %param.14, s32[]{:T(128)S(6)} %axis_index.14), kind=kLoop, calls=%fused_computation.38 | loop fusion | flops 44544 | bytes 21516 | tf_op jit(solution)/shard_map/add | solution.py:496
  4.0 0.6 select_reduce_fusion
  4.6 0.1 reduce_sum.31
  4.7 0.1 slice.26
  4.8 0.7 fusion.7
  5.5 0.1 fusion.15
  5.6 1.3 %copy.16 = bf16[128,12,128]{2,1,0:T(8,128)(2,1)S(1)} copy(bf16[128,12,128]{2,0,1:T(8,128)(2,1)} %param.10) | data formatting | bytes 786432 | tf_op args[0]
  6.9 0.1 pad.27.old
  7.0 0.0 copy-done
  7.0 56.9 %shard_map.82 = (f32[12,256,128]{2,1,0:T(8,128)S(1)}, f32[2,32,128]{2,1,0:T(8,128)S(1)}, f32[2,16,128]{2,1,0:T(8,128)S(1)}, s32[8,128]{1,0:T(8,128)S(1)}) custom-call(s32[1728]{0:T(1024)S(1)} %add_select_fusion.1.picks, s32[9,8,128]{2,1,0:T(8,128)S(1)} %pad.26.labels, s32[8,128]{1,0:T(8,128)S(1)} %broadcast_in_dim.41.over, ...), custom_call_target="tpu_custom_call" | custom-call | flops 905969664 | bytes 12582912 | tf_op jit(solution)/shard_map/pallas_call | solution.py:349
  64.0 0.5 slice.24
  65.1 2.9 %conditional.1 = (f32[12,256,128]{2,1,0:T(8,128)S(1)}) conditional(s32[]{:T(128)} %bitcast.4, (f32[12,256,128]{2,1,0:T(8,128)S(1)}, f32[2,32,128]{2,1,0:T(8,128)S(1)}, f32[2,16,128]{2,1,0:T(8,128)S(1)}, f32[2,256,128]{2,1,0:T(8,128)S(1)}) %tuple.17, (s32[1728]{0:T(1024)S(1)}, s32[9,8,128]{2,1,0:T(8,128)S(1)}, s32[8,128]{1,0:T(8,128)S(1)}, ...), branch_computations={%region_4.5_spmd, %region_5.6_spmd} | conditional | flops 905969664 | bytes 12582920 | solution.py:538
  65.1 2.9 %branch_0_fun.1 = f32[12,256,128]{2,1,0:T(8,128)S(1)} custom-call(f32[12,256,128]{2,1,0:T(8,128)S(1)} %get-tuple-element.28.state, f32[2,32,128]{2,1,0:T(8,128)S(1)} %get-tuple-element.29.halo_y, f32[2,16,128]{2,1,0:T(8,128)S(1)} %get-tuple-element.30.halo_x, f32[2,256,128]{2,1,0:T(8,128)S(1)} %get-tuple-element.31.vel), custom_call_target="tpu_custom_call" | custom-call | tf_op jit(solution)/shard_map/cond/branch_0_fun/pallas_call | solution.py:468
  68.1 0.0 copy-start.1
  68.1 1.1 %copy-done.1 = f32[12,256,128]{2,1,0:T(8,128)} copy-done((f32[12,256,128]{2,1,0:T(8,128)}, f32[12,256,128]{2,1,0:T(8,128)S(1)}, u32[]{:S(2)}) %copy-start.1) | copy-done | bytes 1572888
  (12 shorter events, 0.1 us)
Async XLA Ops:
  0.0 7.0 %copy-start = (f32[2,256,128]{2,1,0:T(8,128)S(1)}, f32[2,256,128]{2,1,0:T(8,128)}, u32[]{:S(2)}) copy-start(f32[2,256,128]{2,1,0:T(8,128)} %vel.1) | copy-start | bytes 786436
  68.1 1.1 %copy-start.1 = (f32[12,256,128]{2,1,0:T(8,128)}, f32[12,256,128]{2,1,0:T(8,128)S(1)}, u32[]{:S(2)}) copy-start(f32[12,256,128]{2,1,0:T(8,128)S(1)} %get-tuple-element.53) | copy-start | bytes 4718596

commit v3 on v2

--- a/solution.py
+++ b/solution.py
@@ -15,10 +15,14 @@
 
 MESH = pl.DeviceIdType.MESH
 CHUNK = 48
+WIDE = 128
 HALO_ROWS = 14
 USUAL = (2, 3, 4)
 FULL = (4, 4, 4)
 MIB = 1 << 20
+
+
+STEPS = ((-1, 1), (-1, -1), (1, 1), (1, -1), (0, 1), (0, -1), (-1, 0), (1, 0), (0, 0))
 
 
 def step_of(k):
@@ -42,6 +46,84 @@
     n = neighbours_of(x, y, nx, ny)
     inner, edge, corner = caps
     return jnp.where(n >= 8, inner, jnp.where(n >= 5, edge, corner))
+
+
+def plan_kernel(
+    nx,
+    ny,
+    caps,
+    send_count,
+    source_block,
+    tile_index,
+    dest_device,
+    dest_block,
+    picks,
+    labels,
+    over_flag,
+):
+    gx, gy = lax.axis_index("gx"), lax.axis_index("gy")
+
+    slots = source_block.shape[1]
+    ids = lax.broadcasted_iota(jnp.int32, (1, slots), 1)
+    place_shift = ny.bit_length() - 1
+    step_x = (dest_device[...] >> place_shift) - gx
+    step_y = (dest_device[...] & (ny - 1)) - gy
+    channel_of = jnp.full((1, slots), 15, jnp.int32)
+    for k, (dx, dy) in enumerate(STEPS):
+        channel_of = jnp.where((step_x == dx) & (step_y == dy), k, channel_of)
+    channel_of = jnp.where(ids < send_count[0], channel_of, 15)
+    matches = channel_of == lax.broadcasted_iota(jnp.int32, (16, slots), 0)
+    matches = matches & (lax.broadcasted_iota(jnp.int32, (16, slots), 0) < 9)
+    ones = jnp.where(matches, 1.0, 0.0)
+    counts = jnp.sum(ones, axis=1, keepdims=True)
+    allowed = (chunks_of(gx, gy, nx, ny, caps) * CHUNK).astype(jnp.float32)
+    over = jnp.max(jnp.where(counts[:8] > allowed, 1.0, 0.0), axis=0, keepdims=True)
+    over_flag[...] = jnp.broadcast_to(over, over_flag.shape)
+    before = lax.broadcasted_iota(jnp.int32, (slots, slots), 0) < lax.broadcasted_iota(
+        jnp.int32, (slots, slots), 1
+    )
+    earlier = jnp.dot(
+        ones.astype(jnp.bfloat16),
+        jnp.where(before, 1.0, 0.0).astype(jnp.bfloat16),
+        preferred_element_type=jnp.float32,
+    )
+    position = jnp.sum(ones * earlier, axis=0, keepdims=True).astype(jnp.int32)
+    place = lax.broadcasted_iota(jnp.int32, (3 * WIDE, slots), 0)
+    place = jnp.where(
+        place < WIDE,
+        jnp.where(place < 2 * CHUNK, place, -1),
+        jnp.where(place % WIDE < CHUNK, place % WIDE + (place // WIDE + 1) * CHUNK, -1),
+    )
+    at_place = jnp.where(place == position, 1.0, 0.0).astype(jnp.bfloat16)
+    tile = tile_index[...]
+    parcels = [source_block[...], tile >> 1, tile & 1, dest_block[...] + 1]
+    parcels = [(ones * v.astype(jnp.float32)).astype(jnp.bfloat16) for v in parcels]
+    ordered = lax.dot_general(
+        jnp.concatenate(parcels, axis=0),
+        at_place,
+        (((1,), (1,)), ((), ())),
+        preferred_element_type=jnp.float32,
+    )
+    picks[...] = (
+        (2.0 * ordered[16:32] + ordered[32:48]) * 128.0 + ordered[0:16]
+    ).astype(jnp.int32)
+    label_rows = ordered[48:64].astype(jnp.int32) - 1
+    for k in range(9):
+        labels[k] = label_rows[k : k + 1]
+
+
+def plan(nx, ny, caps, lists):
+    in_vmem = pl.BlockSpec(memory_space=pltpu.VMEM)
+    return pl.pallas_call(
+        functools.partial(plan_kernel, nx, ny, caps),
+        out_shape=(
+            jax.ShapeDtypeStruct((16, 3 * WIDE), jnp.int32),
+            jax.ShapeDtypeStruct((9, 1, 3 * WIDE), jnp.int32),
+            jax.ShapeDtypeStruct((8, 128), jnp.float32),
+        ),
+        in_specs=[pl.BlockSpec(memory_space=pltpu.SMEM)] + [in_vmem] * 4,
+        out_specs=(in_vmem,) * 3,
+    )(*lists)
 
 
 def mirrored(x, y, nx, ny, t):
@@ -67,6 +149,7 @@
     halo_y,
     halo_x,
     any_over,
+    blocks,
     tiles,
     outgoing,
     incoming,
@@ -128,8 +211,7 @@
         flag_copy(t).wait_recv()
         flags[t + 1] = jnp.maximum(flags[t], flags_in[t])
 
-        @pl.when(t + 1 < swaps)
-        def _():
+        if t + 1 < swaps:
             flag_copy(t + 1).start()
 
     def label_copy(k):
@@ -175,20 +257,30 @@
 
     each_channel(lambda k: label_copy(k).start(), goes_out)
 
+    blocks[...] = jnp.zeros_like(blocks)
+    for c in range(state_count):
+        blocks[:, c, :] = old[c].astype(jnp.float32)
+    for t in range(swaps):
+        pass_flag(t)
     for part in range(parts):
         span = pl.ds(part * depth, depth)
         pltpu.make_async_copy(weights.at[span], tiles.at[span], load_sem.at[part]).wait()
 
     def compute_chunk(k, j):
-        for i in range(CHUNK):
-            pick = picks[k * cap + j * CHUNK + i]
+        at = jnp.where(j < 2, j * CHUNK, (j - 1) * WIDE)
+        none = jnp.zeros((16, 128), jnp.bfloat16)
+        join = jnp.concatenate
+        for i in range(0, CHUNK, 4):
+            four = [picks[k, at + i + n] for n in range(4)]
+            a = [blocks[p & 127].astype(jnp.bfloat16) for p in four]
+            w = [tiles[p >> 7] for p in four]
+            left = join([join([a[n], none] if n % 2 == 0 else [none, a[n]], 1) for n in range(4)], 0)
+            right = join([join([w[0], w[1]], 1), join([w[2], w[3]], 1)], 0)
             piece = lax.dot_general(
-                old[pick & 127],
-                tiles[pick >> 7],
-                (((1,), (1,)), ((), ())),
-                preferred_element_type=jnp.float32,
+                left, right, (((1,), (1,)), ((), ())), preferred_element_type=jnp.float32
             )
-            turn[pl.ds(16 * i, 16), :] = piece
+            turn[pl.ds(16 * i, 32), :] = piece[:32, :128]
+            turn[pl.ds(16 * i + 32, 32), :] = piece[32:, 128:]
         for group in range(CHUNK // 16):
             for c in range(state_count):
                 turned = turn[pl.ds(256 * group + c, 16, stride=16), :]
@@ -208,18 +300,7 @@
 
         lax.fori_loop(0, count, chunk, 0)
 
-    def channel_and_flag(k, carry):
-        @pl.when(goes_out(k))
-        def _():
-            channel(k)
-
-        @pl.when(k < swaps)
-        def _():
-            pass_flag(k)
-
-        return carry
-
-    lax.fori_loop(0, 8, channel_and_flag, 0)
+    each_channel(channel, goes_out)
 
     def own_chunk(j, carry):
         compute_chunk(8, j)
@@ -227,7 +308,7 @@
 
     lax.fori_loop(0, cap // CHUNK, own_chunk, 0)
 
-    row_ids = lax.broadcasted_iota(jnp.int32, (rows, 128), 0)
+    row_ids = lax.broadcasted_iota(jnp.int32, (rows, WIDE), 0)
 
     def add(label_row, values, first):
         width = values.shape[0]
@@ -245,8 +326,10 @@
                 remapped[c] += summed[:, :128]
                 remapped[c + 1] += summed[:, 128:]
 
-    add(labels[8, 0:1, :], outgoing[8, 0 : 2 * CHUNK], True)
-    add(labels[8, 1:2, :], outgoing[8, 2 * CHUNK : 4 * CHUNK], False)
+    add(labels[8, :, :WIDE], outgoing[8, : 2 * CHUNK], True)
+    for j in (2, 3):
+        span = slice((j - 1) * WIDE, j * WIDE)
+        add(labels[8, :, span], outgoing[8, j * CHUNK : (j + 1) * CHUNK], False)
 
     def accept(k):
         dx, dy = step_of(k)
@@ -254,14 +337,14 @@
         label_copy(k).wait_recv()
         chunk_copy(k, 0).wait_recv()
         chunk_copy(k, 1).wait_recv()
-        add(incoming_labels[k, 0:1, :], incoming[k, 0 : 2 * CHUNK], False)
+        add(incoming_labels[k, :, :WIDE], incoming[k, 0 : 2 * CHUNK], False)
         for j in (2, 3):
 
             @pl.when(arriving > j)
             def _():
                 chunk_copy(k, j).wait_recv()
                 add(
-                    incoming_labels[k, j : j + 1, :],
+                    incoming_labels[k, :, (j - 1) * WIDE : j * WIDE],
                     incoming[k, j * CHUNK : (j + 1) * CHUNK],
                     False,
                 )
@@ -341,8 +424,8 @@
 
 def exchange(nx, ny, caps, collective_id, picks, labels, over, old, velocity, weights):
     swaps = nx.bit_length() + ny.bit_length() - 2
-    state_count, rows = HALO_ROWS - 2, velocity.shape[1]
-    cap = labels.shape[2] // 128 * 192
+    state_count, rows = old.shape[0], velocity.shape[1]
+    cap = 4 * CHUNK
     f32, vmem = jnp.float32, pltpu.VMEM
     in_vmem = pl.BlockSpec(memory_space=vmem)
     dma = pltpu.SemaphoreType.DMA
@@ -352,27 +435,23 @@
             jax.ShapeDtypeStruct((state_count, rows, 128), f32),
             jax.ShapeDtypeStruct((2, 32, 128), f32),
             jax.ShapeDtypeStruct((2, 16, 128), f32),
-            jax.ShapeDtypeStruct((8, 128), jnp.int32),
+            jax.ShapeDtypeStruct((8, 128), f32),
         ),
-        in_specs=[
-            pl.BlockSpec(memory_space=pltpu.SMEM),
-            in_vmem,
-            in_vmem,
-            in_vmem,
-            in_vmem,
-            pl.BlockSpec(memory_space=pl.ANY),
-        ],
+        in_specs=[pl.BlockSpec(memory_space=pltpu.SMEM)]
+        + [in_vmem] * 4
+        + [pl.BlockSpec(memory_space=pl.ANY)],
         out_specs=(in_vmem,) * 4,
         scratch_shapes=[
+            vmem((old.shape[1], 16, 128), f32),
             vmem(weights.shape, jnp.bfloat16),
             vmem((9, cap, state_count * 128), jnp.bfloat16),
             vmem((8, cap, state_count * 128), jnp.bfloat16),
-            vmem((8, 8, 128), jnp.int32),
+            vmem((8, 1, 3 * WIDE), jnp.int32),
             vmem((16 * CHUNK, 128), f32),
             vmem((4, 32, 128), f32),
             vmem((4, 16, 128), f32),
-            vmem((swaps + 1, 8, 128), jnp.int32),
-            vmem((swaps, 8, 128), jnp.int32),
+            vmem((swaps + 1, 8, 128), f32),
+            vmem((swaps, 8, 128), f32),
             dma((4,)),
             dma((2, 8)),
             dma((8, cap // CHUNK)),
@@ -384,7 +463,7 @@
             collective_id=collective_id, has_side_effects=True, vmem_limit_bytes=48 * MIB
         ),
         cost_estimate=pl.CostEstimate(
-            flops=2 * picks.shape[0] * 128 * 128 * 16,
+            flops=2 * 9 * cap * 128 * 128 * 16,
             bytes_accessed=weights.size * 2,
             transcendentals=0,
         ),
@@ -475,39 +554,6 @@
     )(state, halo_y, halo_x, velocity)
 
 
-def plan(source_block, tile_index, dest_device, dest_block, send_count, caps, nx, ny):
-    slots = source_block.shape[0]
-    cap = slots // 4
-    live = jnp.arange(slots) < send_count[0]
-    sx = dest_device // ny - lax.axis_index("gx")
-    sy = dest_device % ny - lax.axis_index("gy")
-    m = jnp.where(sx == 0, 2, (sx + 1) // 2)
-    channel = jnp.where(sy == 0, jnp.where(sx == 0, 8, 6 + (sx + 1) // 2), 2 * m + (sy < 0))
-    channel = jnp.where(live, channel, 9)
-    matches = channel[None, :] == jnp.arange(9)[:, None]
-    earlier = jnp.arange(slots)[:, None] < jnp.arange(slots)[None, :]
-    position = jnp.dot(
-        matches.astype(jnp.bfloat16),
-        earlier.astype(jnp.bfloat16),
-        preferred_element_type=jnp.float32,
-    )
-    position = jnp.sum(jnp.where(matches, position, 0.0), axis=0).astype(jnp.int32)
-    target = jnp.where(live, channel * cap + position, -1)
-    value = (tile_index * 128 + source_block) * 512 + dest_block + 1
-    value = jnp.sum(
-        jnp.where(target[None, :] == jnp.arange(9 * cap)[:, None], value[None, :], 0), axis=1
-    )
-    rows = (value % 512 - 1).reshape(9, cap)
-    half, quarter = cap // 2, cap // 4
-    pieces = (rows[:, :half], rows[:, half:], rows[:, half : half + quarter], rows[:, half + quarter :])
-    pieces = [jnp.pad(p, ((0, 0), (0, 128 - p.shape[1]))) for p in pieces]
-    labels = jnp.pad(jnp.stack(pieces, axis=1), ((0, 0), (0, 4), (0, 0)))
-    counts = jnp.sum(matches.astype(jnp.int32), axis=1)[:8]
-    allowed = chunks_of(lax.axis_index("gx"), lax.axis_index("gy"), nx, ny, caps) * CHUNK
-    over = jnp.broadcast_to((jnp.max(counts) > allowed).astype(jnp.int32), (8, 128))
-    return value // 512, labels, over
-
-
 def per_device(
     nx,
     ny,
@@ -520,16 +566,15 @@
     send_count,
     velocity,
 ):
-    picks, labels, over = plan(
-        source_block, tile_index, dest_device, dest_block, send_count, USUAL, nx, ny
-    )
-    old = jnp.pad(old_states, ((0, 0), (0, 4), (0, 0)))
-    *edges, any_over = exchange(
-        nx, ny, USUAL, 0, picks, labels, over, old, velocity, weight_tiles
-    )
+    lists = [send_count] + [
+        v.reshape(1, -1) for v in (source_block, tile_index, dest_device, dest_block)
+    ]
+    old = jnp.transpose(old_states, (1, 0, 2))
+    places = plan(nx, ny, USUAL, lists)
+    *edges, any_over = exchange(nx, ny, USUAL, 0, *places, old, velocity, weight_tiles)
 
     def again(*_):
-        *edges, _ = exchange(nx, ny, FULL, 1, picks, labels, over, old, velocity, weight_tiles)
+        *edges, _ = exchange(nx, ny, FULL, 1, *places, old, velocity, weight_tiles)
         return advance(*edges, velocity)
 
     def enough(*edges):

time: 69.5 us -> 71.6 us (1.030)
  the two profiles are of different devices: /device:TPU:24 before, /device:TPU:0 now
where the time goes in v3:
time: 71.6 us; the launch traced here: 71.1 us
  Pallas kernels  63 us (88%)
  local copies, waits for them, and re-layouts  6.74 us (9%)
  between operations  1.37 us (2%)
    pallas_call x1, Pallas kernels, exchange(): pl.pallas_call(functools.partial(exchange_kernel, nx, ny, caps), out_shap...  58.8 us
    reshape x4, local copies, waits for them, and re-layouts, per_device(): v.reshape(1, -1)  5.08 us
    pallas_call x1, Pallas kernels, advance(): pl.pallas_call(step_kernel, grid=(rows // 32,), out_shape=jax.ShapeDtypeS...  2.91 us

profile of v3, /device:TPU:0, one launch (start us, length us, event | category | flops | bytes accessed | tf_op | source)
XLA Modules:
  0.0 71.1 jit_solution(17688888094248316525)
XLA Ops:
  0.7 1.3 %reshape.16.source_block = s32[1,768]{1,0:T(1,128)} reshape(s32[768]{0:T(1024)} %param.12) | data formatting | bytes 6144 | tf_op jit(solution)/shard_map/reshape | solution.py:570
  1.9 1.3 %reshape.17.tile_index = s32[1,768]{1,0:T(1,128)} reshape(s32[768]{0:T(1024)} %param.13) | data formatting | bytes 6144 | tf_op jit(solution)/shard_map/reshape | solution.py:570
  3.2 1.2 %reshape.18.dest_device = s32[1,768]{1,0:T(1,128)} reshape(s32[768]{0:T(1024)} %param.14) | data formatting | bytes 6144 | tf_op jit(solution)/shard_map/reshape | solution.py:570
  4.5 1.3 %reshape.19.dest_block = s32[1,768]{1,0:T(1,128)} reshape(s32[768]{0:T(1024)} %param.15) | data formatting | bytes 6144 | tf_op jit(solution)/shard_map/reshape | solution.py:570
  5.7 1.2 %shard_map.82 = (s32[16,384]{1,0:T(8,128)S(1)}, s32[9,1,384]{2,1,0:T(1,128)S(1)}, f32[8,128]{1,0:T(8,128)S(1)}) custom-call(s32[1]{0:T(128)S(6)} %copy.11.send_count, s32[1,768]{1,0:T(1,128)} %reshape.16.source_block, s32[1,768]{1,0:T(1,128)} %reshape.17.tile_index, s32[1,768]{1,0:T(1,128)} %reshape.18.dest_device, s32[1,768]{1,0:T(1,128)} %reshape.19.dest_block), custom_call_target="tpu_custom_call" | custom-call | tf_op jit(solution)/shard_map/pallas_call | solution.py:117
  7.0 0.0 copy-start
  7.0 0.0 copy-start.1
  7.0 58.8 %shard_map.83 = (f32[12,256,128]{2,1,0:T(8,128)S(1)}, f32[2,32,128]{2,1,0:T(8,128)S(1)}, f32[2,16,128]{2,1,0:T(8,128)S(1)}, f32[8,128]{1,0:T(8,128)S(1)}) custom-call(s32[16,384]{1,0:T(8,128)S(1)} %get-tuple-element.48.picks, s32[9,1,384]{2,1,0:T(1,128)S(1)} %get-tuple-element.49.labels, f32[8,128]{1,0:T(8,128)S(1)} %get-tuple-element.50.over, ...), custom_call_target="tpu_custom_call" | custom-call | flops 905969664 | bytes 12582912 | tf_op jit(solution)/shard_map/pallas_call | solution.py:432
  65.8 0.5 slice.3
  67.0 0.0 copy-done
  67.0 0.0 copy-done.1
  67.0 2.9 %conditional.1 = (f32[12,256,128]{2,1,0:T(8,128)S(1)}) conditional(s32[]{:T(128)} %bitcast.1, (f32[12,256,128]{2,1,0:T(8,128)S(1)}, f32[2,32,128]{2,1,0:T(8,128)S(1)}, f32[2,16,128]{2,1,0:T(8,128)S(1)}, f32[2,256,128]{2,1,0:T(8,128)S(1)}) %tuple.15, (s32[16,384]{1,0:T(8,128)S(1)}, s32[9,1,384]{2,1,0:T(1,128)S(1)}, f32[8,128]{1,0:T(8,128)S(1)}, ...), branch_computations={%region_0.0_spmd, %region_1.0_spmd} | conditional | flops 905969664 | bytes 12582920 | solution.py:583
  67.0 2.9 %branch_0_fun.1 = f32[12,256,128]{2,1,0:T(8,128)S(1)} custom-call(f32[12,256,128]{2,1,0:T(8,128)S(1)} %get-tuple-element.28.state, f32[2,32,128]{2,1,0:T(8,128)S(1)} %get-tuple-element.29.halo_y, f32[2,16,128]{2,1,0:T(8,128)S(1)} %get-tuple-element.30.halo_x, f32[2,256,128]{2,1,0:T(8,128)S(1)} %get-tuple-element.31.vel), custom_call_target="tpu_custom_call" | custom-call | tf_op jit(solution)/shard_map/cond/branch_0_fun/pallas_call | solution.py:547
  70.0 0.0 copy-start.2
  70.0 1.1 %copy-done.2 = f32[12,256,128]{2,1,0:T(8,128)} copy-done((f32[12,256,128]{2,1,0:T(8,128)}, f32[12,256,128]{2,1,0:T(8,128)S(1)}, u32[]{:S(2)}) %copy-start.2) | copy-done | bytes 1572888
Async XLA Ops:
  7.0 60.0 %copy-start = (f32[2,256,128]{2,1,0:T(8,128)S(1)}, f32[2,256,128]{2,1,0:T(8,128)}, u32[]{:S(2)}) copy-start(f32[2,256,128]{2,1,0:T(8,128)} %vel.1) | copy-start | bytes 786436
  7.0 60.0 %copy-start.1 = (bf16[128,12,128]{2,0,1:T(8,128)(2,1)S(1)}, bf16[128,12,128]{2,0,1:T(8,128)(2,1)}, u32[]{:S(2)}) copy-start(bf16[128,12,128]{2,0,1:T(8,128)(2,1)} %param.10) | copy-start | bytes 1179652
  70.0 1.1 %copy-start.2 = (f32[12,256,128]{2,1,0:T(8,128)}, f32[12,256,128]{2,1,0:T(8,128)S(1)}, u32[]{:S(2)}) copy-start(f32[12,256,128]{2,1,0:T(8,128)S(1)} %get-tuple-element.55) | copy-start | bytes 4718596

commit v4 on v3

--- a/solution.py
+++ b/solution.py
@@ -14,11 +14,13 @@
 fiber_number = 2.0
 
 MESH = pl.DeviceIdType.MESH
-CHUNK = 48
+CHUNK = 32
 WIDE = 128
+FIRST = 3
+CHUNKS = 6
 HALO_ROWS = 14
-USUAL = (2, 3, 4)
-FULL = (4, 4, 4)
+USUAL = (3, 4, 5, 6)
+FULL = (6, 6, 6, 6)
 MIB = 1 << 20
 
 
@@ -42,10 +44,11 @@
     return spread_x * spread_y - 1
 
 
-def chunks_of(x, y, nx, ny, caps):
+def chunks_of(x, y, dy, nx, ny, caps):
     n = neighbours_of(x, y, nx, ny)
-    inner, edge, corner = caps
-    return jnp.where(n >= 8, inner, jnp.where(n >= 5, edge, corner))
+    inner, along, edge, corner = caps
+    sidewise = jnp.where((dy != 0) & ((y == 0) | (y == ny - 1)), along, edge)
+    return jnp.where(n >= 8, inner, jnp.where(n >= 5, sidewise, corner))
 
 
 def plan_kernel(
@@ -63,11 +66,12 @@
 ):
     gx, gy = lax.axis_index("gx"), lax.axis_index("gy")
 
-    slots = source_block.shape[1]
+    slots = source_block.shape[0]
+    dest, tile = dest_device[...].reshape(1, slots), tile_index[...].reshape(1, slots)
     ids = lax.broadcasted_iota(jnp.int32, (1, slots), 1)
     place_shift = ny.bit_length() - 1
-    step_x = (dest_device[...] >> place_shift) - gx
-    step_y = (dest_device[...] & (ny - 1)) - gy
+    step_x = (dest >> place_shift) - gx
+    step_y = (dest & (ny - 1)) - gy
     channel_of = jnp.full((1, slots), 15, jnp.int32)
     for k, (dx, dy) in enumerate(STEPS):
         channel_of = jnp.where((step_x == dx) & (step_y == dy), k, channel_of)
@@ -76,8 +80,10 @@
     matches = matches & (lax.broadcasted_iota(jnp.int32, (16, slots), 0) < 9)
     ones = jnp.where(matches, 1.0, 0.0)
     counts = jnp.sum(ones, axis=1, keepdims=True)
-    allowed = (chunks_of(gx, gy, nx, ny, caps) * CHUNK).astype(jnp.float32)
-    over = jnp.max(jnp.where(counts[:8] > allowed, 1.0, 0.0), axis=0, keepdims=True)
+    over = jnp.zeros((1, 1), jnp.float32)
+    for k, (_, dy) in enumerate(STEPS[:8]):
+        allowed = (chunks_of(gx, gy, dy, nx, ny, caps) * CHUNK).astype(jnp.float32)
+        over = jnp.maximum(over, jnp.where(counts[k : k + 1] > allowed, 1.0, 0.0))
     over_flag[...] = jnp.broadcast_to(over, over_flag.shape)
     before = lax.broadcasted_iota(jnp.int32, (slots, slots), 0) < lax.broadcasted_iota(
         jnp.int32, (slots, slots), 1
@@ -88,15 +94,15 @@
         preferred_element_type=jnp.float32,
     )
     position = jnp.sum(ones * earlier, axis=0, keepdims=True).astype(jnp.int32)
-    place = lax.broadcasted_iota(jnp.int32, (3 * WIDE, slots), 0)
+    place = lax.broadcasted_iota(jnp.int32, (4 * WIDE, slots), 0)
     place = jnp.where(
         place < WIDE,
-        jnp.where(place < 2 * CHUNK, place, -1),
-        jnp.where(place % WIDE < CHUNK, place % WIDE + (place // WIDE + 1) * CHUNK, -1),
+        jnp.where(place < FIRST * CHUNK, place, -1),
+        jnp.where(place % WIDE < CHUNK, place % WIDE + (place // WIDE + FIRST - 1) * CHUNK, -1),
     )
     at_place = jnp.where(place == position, 1.0, 0.0).astype(jnp.bfloat16)
-    tile = tile_index[...]
-    parcels = [source_block[...], tile >> 1, tile & 1, dest_block[...] + 1]
+    source, row = source_block[...].reshape(1, slots), dest_block[...].reshape(1, slots)
+    parcels = [source, tile >> 1, tile & 1, row + 1]
     parcels = [(ones * v.astype(jnp.float32)).astype(jnp.bfloat16) for v in parcels]
     ordered = lax.dot_general(
         jnp.concatenate(parcels, axis=0),
@@ -117,22 +123,13 @@
     return pl.pallas_call(
         functools.partial(plan_kernel, nx, ny, caps),
         out_shape=(
-            jax.ShapeDtypeStruct((16, 3 * WIDE), jnp.int32),
-            jax.ShapeDtypeStruct((9, 1, 3 * WIDE), jnp.int32),
-            jax.ShapeDtypeStruct((8, 128), jnp.float32),
+            jax.ShapeDtypeStruct((16, 4 * WIDE), jnp.int32),
+            jax.ShapeDtypeStruct((9, 1, 4 * WIDE), jnp.int32),
+            jax.ShapeDtypeStruct((1, 128), jnp.float32),
         ),
         in_specs=[pl.BlockSpec(memory_space=pltpu.SMEM)] + [in_vmem] * 4,
         out_specs=(in_vmem,) * 3,
     )(*lists)
-
-
-def mirrored(x, y, nx, ny, t):
-    bits_x = nx.bit_length() - 1
-    for step in range(bits_x):
-        x = jnp.where(t == step, x + (1 - 2 * (x // 2**step % 2)) * 2**step, x)
-    for step in range(ny.bit_length() - 1):
-        y = jnp.where(t == bits_x + step, y + (1 - 2 * (y // 2**step % 2)) * 2**step, y)
-    return x, y
 
 
 def exchange_kernel(
@@ -187,32 +184,55 @@
                 barrier, inc=1, device_id=(gx + dx, gy + dy), device_id_type=MESH
             )
 
-    swaps = flags_in.shape[0]
-    for t in range(swaps):
-        pl.semaphore_signal(
-            barrier, inc=1, device_id=mirrored(gx, gy, nx, ny, t), device_id_type=MESH
-        )
-    pl.semaphore_wait(barrier, neighbours_of(gx, gy, nx, ny) + swaps)
-
-    def flag_copy(t):
+
+    def along_gx(j):
+        return (lax.rem(gx + j, nx), gy)
+
+    def along_gy(j):
+        return (gx, lax.rem(gy + j, ny))
+
+    def greet(j, carry, along):
+        pl.semaphore_signal(barrier, inc=1, device_id=along(j), device_id_type=MESH)
+        return carry
+
+    lax.fori_loop(1, nx, functools.partial(greet, along=along_gx), 0)
+    lax.fori_loop(1, ny, functools.partial(greet, along=along_gy), 0)
+    pl.semaphore_wait(barrier, neighbours_of(gx, gy, nx, ny) + nx + ny - 2)
+
+    def flag_copy(turn_of, j):
+        slot = turn_of * nx + j
         return pltpu.make_async_remote_copy(
-            src_ref=flags.at[t],
-            dst_ref=flags_in.at[t],
-            send_sem=flag_sems.at[0, t],
-            recv_sem=flag_sems.at[1, t],
-            device_id=mirrored(gx, gy, nx, ny, t),
+            src_ref=flags.at[turn_of],
+            dst_ref=flags_in.at[slot],
+            send_sem=flag_sems.at[0, slot],
+            recv_sem=flag_sems.at[1, slot],
+            device_id=(along_gx, along_gy)[turn_of](j),
             device_id_type=MESH,
         )
 
+    def send_flag(turn_of):
+        def step(j, carry):
+            flag_copy(turn_of, j).start()
+            return carry
+
+        lax.fori_loop(1, (nx, ny)[turn_of], step, 0)
+
+    def gather_flag(turn_of):
+        def step(j, carry):
+            flag_copy(turn_of, j).wait_recv()
+            return jnp.maximum(carry, flags_in[turn_of * nx + j])
+
+        flags[turn_of + 1] = lax.fori_loop(1, (nx, ny)[turn_of], step, flags[turn_of])
+
+    def end_flag(turn_of):
+        def step(j, carry):
+            flag_copy(turn_of, j).wait_send()
+            return carry
+
+        lax.fori_loop(1, (nx, ny)[turn_of], step, 0)
+
     flags[0] = over[...]
-    flag_copy(0).start()
-
-    def pass_flag(t):
-        flag_copy(t).wait_recv()
-        flags[t + 1] = jnp.maximum(flags[t], flags_in[t])
-
-        if t + 1 < swaps:
-            flag_copy(t + 1).start()
+    send_flag(0)
 
     def label_copy(k):
         dx, dy = step_of(k)
@@ -260,14 +280,12 @@
     blocks[...] = jnp.zeros_like(blocks)
     for c in range(state_count):
         blocks[:, c, :] = old[c].astype(jnp.float32)
-    for t in range(swaps):
-        pass_flag(t)
     for part in range(parts):
         span = pl.ds(part * depth, depth)
         pltpu.make_async_copy(weights.at[span], tiles.at[span], load_sem.at[part]).wait()
 
     def compute_chunk(k, j):
-        at = jnp.where(j < 2, j * CHUNK, (j - 1) * WIDE)
+        at = jnp.where(j < FIRST, j * CHUNK, (j - FIRST + 1) * WIDE)
         none = jnp.zeros((16, 128), jnp.bfloat16)
         join = jnp.concatenate
         for i in range(0, CHUNK, 4):
@@ -290,23 +308,32 @@
                     pl.ds(c * 128, 128),
                 ] = turned.astype(jnp.bfloat16)
 
-    count = chunks_of(gx, gy, nx, ny, caps)
-
-    def channel(k):
+    def sent(k):
+        _, dy = step_of(k)
+        return chunks_of(gx, gy, dy, nx, ny, caps)
+
+    def channel(k, carry):
         def chunk(j, carry):
             compute_chunk(k, j)
-            chunk_copy(k, j).start()
+
+            @pl.when(k < 8)
+            def _():
+                chunk_copy(k, j).start()
+
             return carry
 
-        lax.fori_loop(0, count, chunk, 0)
-
-    each_channel(channel, goes_out)
-
-    def own_chunk(j, carry):
-        compute_chunk(8, j)
+        @pl.when((k == 8) | goes_out(k))
+        def _():
+            lax.fori_loop(0, jnp.where(k == 8, CHUNKS, sent(k)), chunk, 0)
+
+        @pl.when(k == 1)
+        def _():
+            gather_flag(0)
+            send_flag(1)
+
         return carry
 
-    lax.fori_loop(0, cap // CHUNK, own_chunk, 0)
+    lax.fori_loop(0, 9, channel, 0)
 
     row_ids = lax.broadcasted_iota(jnp.int32, (rows, WIDE), 0)
 
@@ -326,28 +353,30 @@
                 remapped[c] += summed[:, :128]
                 remapped[c + 1] += summed[:, 128:]
 
-    add(labels[8, :, :WIDE], outgoing[8, : 2 * CHUNK], True)
-    for j in (2, 3):
-        span = slice((j - 1) * WIDE, j * WIDE)
-        add(labels[8, :, span], outgoing[8, j * CHUNK : (j + 1) * CHUNK], False)
+    def add_piece(label_rows, k, values, first):
+        add(label_rows[k, :, :WIDE], values[k, : FIRST * CHUNK], first)
+
+    def add_chunk(label_rows, k, values, j):
+        lanes_of = slice((j - FIRST + 1) * WIDE, (j - FIRST + 2) * WIDE)
+        add(label_rows[k, :, lanes_of], values[k, j * CHUNK : (j + 1) * CHUNK], False)
+
+    add_piece(labels, 8, outgoing, True)
+    for j in range(FIRST, CHUNKS):
+        add_chunk(labels, 8, outgoing, j)
 
     def accept(k):
         dx, dy = step_of(k)
-        arriving = chunks_of(gx - dx, gy - dy, nx, ny, caps)
+        arriving = chunks_of(gx - dx, gy - dy, dy, nx, ny, caps)
         label_copy(k).wait_recv()
-        chunk_copy(k, 0).wait_recv()
-        chunk_copy(k, 1).wait_recv()
-        add(incoming_labels[k, :, :WIDE], incoming[k, 0 : 2 * CHUNK], False)
-        for j in (2, 3):
+        for j in range(FIRST):
+            chunk_copy(k, j).wait_recv()
+        add_piece(incoming_labels, k, incoming, False)
+        for j in range(FIRST, CHUNKS):
 
             @pl.when(arriving > j)
             def _():
                 chunk_copy(k, j).wait_recv()
-                add(
-                    incoming_labels[k, :, (j - 1) * WIDE : j * WIDE],
-                    incoming[k, j * CHUNK : (j + 1) * CHUNK],
-                    False,
-                )
+                add_chunk(incoming_labels, k, incoming, j)
 
     each_channel(accept, comes_in)
 
@@ -414,18 +443,18 @@
             chunk_copy(k, j).wait_send()
             return carry
 
-        lax.fori_loop(0, count, chunk, 0)
+        lax.fori_loop(0, sent(k), chunk, 0)
 
     each_channel(finish, goes_out)
-    for t in range(swaps):
-        flag_copy(t).wait_send()
-    any_over[...] = flags[swaps]
+    gather_flag(1)
+    end_flag(0)
+    end_flag(1)
+    any_over[...] = flags[2]
 
 
 def exchange(nx, ny, caps, collective_id, picks, labels, over, old, velocity, weights):
-    swaps = nx.bit_length() + ny.bit_length() - 2
     state_count, rows = old.shape[0], velocity.shape[1]
-    cap = 4 * CHUNK
+    cap = CHUNKS * CHUNK
     f32, vmem = jnp.float32, pltpu.VMEM
     in_vmem = pl.BlockSpec(memory_space=vmem)
     dma = pltpu.SemaphoreType.DMA
@@ -435,7 +464,7 @@
             jax.ShapeDtypeStruct((state_count, rows, 128), f32),
             jax.ShapeDtypeStruct((2, 32, 128), f32),
             jax.ShapeDtypeStruct((2, 16, 128), f32),
-            jax.ShapeDtypeStruct((8, 128), f32),
+            jax.ShapeDtypeStruct((1, 128), f32),
         ),
         in_specs=[pl.BlockSpec(memory_space=pltpu.SMEM)]
         + [in_vmem] * 4
@@ -446,18 +475,18 @@
             vmem(weights.shape, jnp.bfloat16),
             vmem((9, cap, state_count * 128), jnp.bfloat16),
             vmem((8, cap, state_count * 128), jnp.bfloat16),
-            vmem((8, 1, 3 * WIDE), jnp.int32),
+            vmem((8, 1, 4 * WIDE), jnp.int32),
             vmem((16 * CHUNK, 128), f32),
             vmem((4, 32, 128), f32),
             vmem((4, 16, 128), f32),
-            vmem((swaps + 1, 8, 128), f32),
-            vmem((swaps, 8, 128), f32),
+            vmem((3, 1, 128), f32),
+            vmem((nx + ny, 1, 128), f32),
             dma((4,)),
             dma((2, 8)),
             dma((8, cap // CHUNK)),
             dma((8, cap // CHUNK)),
             dma((2, 4)),
-            dma((2, swaps)),
+            dma((2, nx + ny)),
         ],
         compiler_params=pltpu.CompilerParams(
             collective_id=collective_id, has_side_effects=True, vmem_limit_bytes=48 * MIB
@@ -566,9 +595,7 @@
     send_count,
     velocity,
 ):
-    lists = [send_count] + [
-        v.reshape(1, -1) for v in (source_block, tile_index, dest_device, dest_block)
-    ]
+    lists = (send_count, source_block, tile_index, dest_device, dest_block)
     old = jnp.transpose(old_states, (1, 0, 2))
     places = plan(nx, ny, USUAL, lists)
     *edges, any_over = exchange(nx, ny, USUAL, 0, *places, old, velocity, weight_tiles)

time: 71.6 us -> 50.1 us (0.70)
  Pallas kernels: 63 us -> 48 us
  local copies, waits for them, and re-layouts: 6.74 us -> 1.15 us
    pallas_call x1, Pallas kernels: 58.8 us -> 43.8 us  [exchange(): pl.pallas_call(functools.partial(exchange_kernel, nx, ny, caps), out_shap...]
    reshape x4 -> x0, local copies, waits for them, and re-layouts: 5.08 us -> none  [per_device(): v.reshape(1, -1)]
where the time goes in v4:
time: 50.1 us; the launch traced here: 50 us
  Pallas kernels  48 us (96%)
  local copies, waits for them, and re-layouts  1.15 us (2%)
  between operations  0.75 us (1%)
    pallas_call x1, Pallas kernels, exchange(): pl.pallas_call(functools.partial(exchange_kernel, nx, ny, caps), out_shap...  43.8 us
    pallas_call x1, Pallas kernels, advance(): pl.pallas_call(step_kernel, grid=(rows // 32,), out_shape=jax.ShapeDtypeS...  2.92 us
    pallas_call x1, Pallas kernels, plan(): pl.pallas_call(functools.partial(plan_kernel, nx, ny, caps), out_shape=(j...  1.27 us
    unnamed x6, local copies, waits for them, and re-layouts  1.15 us

profile of v4, /device:TPU:0, one launch (start us, length us, event | category | flops | bytes accessed | tf_op | source)
XLA Modules:
  0.0 50.0 jit_solution(1872503451275384862)
XLA Ops:
  0.7 1.3 %shard_map.82 = (s32[16,512]{1,0:T(8,128)S(1)}, s32[9,1,512]{2,1,0:T(1,128)S(1)}, f32[1,128]{1,0:T(1,128)S(1)}) custom-call(s32[1]{0:T(128)S(6)} %copy.11.send_count, s32[768]{0:T(1024)} %source_block.1, s32[768]{0:T(1024)} %tile_index.1, s32[768]{0:T(1024)} %dest_device.1, s32[768]{0:T(1024)} %dest_block.1), custom_call_target="tpu_custom_call" | custom-call | tf_op jit(solution)/shard_map/pallas_call | solution.py:123
  1.9 0.0 copy-start
  1.9 0.0 copy-start.1
  2.0 43.8 %shard_map.83 = (f32[12,256,128]{2,1,0:T(8,128)S(1)}, f32[2,32,128]{2,1,0:T(8,128)S(1)}, f32[2,16,128]{2,1,0:T(8,128)S(1)}, f32[1,128]{1,0:T(1,128)S(1)}) custom-call(s32[16,512]{1,0:T(8,128)S(1)} %get-tuple-element.48.picks, s32[9,1,512]{2,1,0:T(1,128)S(1)} %get-tuple-element.49.labels, f32[1,128]{1,0:T(1,128)S(1)} %get-tuple-element.50.over, ...), custom_call_target="tpu_custom_call" | custom-call | flops 905969664 | bytes 12582912 | tf_op jit(solution)/shard_map/pallas_call | solution.py:461
  45.9 0.0 copy-done
  45.9 0.0 copy-done.1
  45.9 2.9 %conditional.1 = (f32[12,256,128]{2,1,0:T(8,128)S(1)}) conditional(s32[]{:T(128)} %bitcast.1, (f32[12,256,128]{2,1,0:T(8,128)S(1)}, f32[2,32,128]{2,1,0:T(8,128)S(1)}, f32[2,16,128]{2,1,0:T(8,128)S(1)}, f32[2,256,128]{2,1,0:T(8,128)S(1)}) %tuple.15, (s32[16,512]{1,0:T(8,128)S(1)}, s32[9,1,512]{2,1,0:T(1,128)S(1)}, f32[1,128]{1,0:T(1,128)S(1)}, ...), branch_computations={%region_0.0_spmd, %region_1.0_spmd} | conditional | flops 905969664 | bytes 12582920 | solution.py:610
  45.9 2.9 %branch_0_fun.1 = f32[12,256,128]{2,1,0:T(8,128)S(1)} custom-call(f32[12,256,128]{2,1,0:T(8,128)S(1)} %get-tuple-element.28.state, f32[2,32,128]{2,1,0:T(8,128)S(1)} %get-tuple-element.29.halo_y, f32[2,16,128]{2,1,0:T(8,128)S(1)} %get-tuple-element.30.halo_x, f32[2,256,128]{2,1,0:T(8,128)S(1)} %get-tuple-element.31.vel), custom_call_target="tpu_custom_call" | custom-call | tf_op jit(solution)/shard_map/cond/branch_0_fun/pallas_call | solution.py:576
  48.8 0.0 copy-start.2
  48.8 1.1 %copy-done.2 = f32[12,256,128]{2,1,0:T(8,128)} copy-done((f32[12,256,128]{2,1,0:T(8,128)}, f32[12,256,128]{2,1,0:T(8,128)S(1)}, u32[]{:S(2)}) %copy-start.2) | copy-done | bytes 1572888
Async XLA Ops:
  1.9 43.9 %copy-start = (f32[2,256,128]{2,1,0:T(8,128)S(1)}, f32[2,256,128]{2,1,0:T(8,128)}, u32[]{:S(2)}) copy-start(f32[2,256,128]{2,1,0:T(8,128)} %vel.1) | copy-start | bytes 786436
  1.9 43.9 %copy-start.1 = (bf16[128,12,128]{2,0,1:T(8,128)(2,1)S(1)}, bf16[128,12,128]{2,0,1:T(8,128)(2,1)}, u32[]{:S(2)}) copy-start(bf16[128,12,128]{2,0,1:T(8,128)(2,1)} %param.10) | copy-start | bytes 1179652
  48.8 1.1 %copy-start.2 = (f32[12,256,128]{2,1,0:T(8,128)}, f32[12,256,128]{2,1,0:T(8,128)S(1)}, u32[]{:S(2)}) copy-start(f32[12,256,128]{2,1,0:T(8,128)S(1)} %get-tuple-element.55) | copy-start | bytes 4718596

commit v5 on v4

--- a/solution.py
+++ b/solution.py
@@ -18,7 +18,6 @@
 WIDE = 128
 FIRST = 3
 CHUNKS = 6
-HALO_ROWS = 14
 USUAL = (3, 4, 5, 6)
 FULL = (6, 6, 6, 6)
 MIB = 1 << 20
@@ -142,10 +141,9 @@
     old,
     vel,
     weights,
+    out,
+    any_over,
     remapped,
-    halo_y,
-    halo_x,
-    any_over,
     blocks,
     tiles,
     outgoing,
@@ -154,6 +152,8 @@
     turn,
     edge_y,
     edge_x,
+    flow_y,
+    flow_x,
     flags,
     flags_in,
     load_sem,
@@ -161,14 +161,14 @@
     send_sems,
     recv_sems,
     edge_sems,
+    flow_sems,
     flag_sems,
 ):
     gx, gy = lax.axis_index("gx"), lax.axis_index("gy")
     parts = load_sem.shape[0]
     depth = tiles.shape[0] // parts
     cap = outgoing.shape[1]
-    rows = remapped.shape[1]
-    state_count = remapped.shape[0]
+    state_count, rows = remapped.shape[:2]
 
     for part in range(parts):
         span = pl.ds(part * depth, depth)
@@ -276,6 +276,47 @@
         lax.fori_loop(0, 8, step, 0)
 
     each_channel(lambda k: label_copy(k).start(), goes_out)
+
+    lanes = lax.broadcasted_iota(jnp.int32, (32, 128), 1)
+    sides = ((0, 0, 1), (1, 0, -1), (0, 1, 0), (1, -1, 0))
+
+    def pack_edges(ref, along_y, along_x):
+        planes = ref.shape[0]
+        for side, lane in ((0, 127), (1, 0)):
+            packed = jnp.zeros((32, 128), jnp.float32)
+            for b in range(rows // 32):
+                for c in range(planes):
+                    to = 16 * b + c
+                    moved = pltpu.roll(ref[c, pl.ds(32 * b, 32), :], (to - lane) % 128, 1)
+                    packed = jnp.where(lanes == to, moved, packed)
+            along_y[side] = packed
+        for side, row in ((0, rows - 1), (1, 0)):
+            for c in range(planes):
+                along_x[side, c : c + 1, :] = ref[c, row : row + 1, :]
+
+    def side_copy(index, along_y, along_x, sems):
+        side, dx, dy = sides[index]
+        edge = along_y if dx == 0 else along_x
+        return pltpu.make_async_remote_copy(
+            src_ref=edge.at[side],
+            dst_ref=edge.at[side + 2],
+            send_sem=sems.at[0, index],
+            recv_sem=sems.at[1, index],
+            device_id=(gx + dx, gy + dy),
+            device_id_type=MESH,
+        )
+
+    def each_side(body, sign):
+        for index, (_, dx, dy) in enumerate(sides):
+
+            @pl.when(exists(gx + sign * dx, gy + sign * dy, nx, ny))
+            def _():
+                body(index)
+
+    flow = (flow_y, flow_x, flow_sems)
+    edges = (edge_y, edge_x, edge_sems)
+    pack_edges(vel, flow_y, flow_x)
+    each_side(lambda index: side_copy(index, *flow).start(), 1)
 
     blocks[...] = jnp.zeros_like(blocks)
     for c in range(state_count):
@@ -378,63 +419,60 @@
                 chunk_copy(k, j).wait_recv()
                 add_chunk(incoming_labels, k, incoming, j)
 
-    each_channel(accept, comes_in)
-
-    lanes = lax.broadcasted_iota(jnp.int32, (32, 128), 1)
-    for side, lane in ((0, 127), (1, 0)):
-        packed = jnp.zeros((32, 128), jnp.float32)
-        for b in range(rows // 32):
-            for c in range(HALO_ROWS):
-                ref = remapped.at[c] if c < state_count else vel.at[c - state_count]
-                to = 16 * b + c
-                moved = pltpu.roll(ref[pl.ds(32 * b, 32), :], (to - lane) % 128, 1)
-                packed = jnp.where(lanes == to, moved, packed)
-        edge_y[side] = packed
-    for side, row in ((0, rows - 1), (1, 0)):
-        for c in range(HALO_ROWS):
-            ref = remapped.at[c] if c < state_count else vel.at[c - state_count]
-            edge_x[side, c : c + 1, :] = ref[row : row + 1, :]
-    sides = (
-        (edge_y, halo_y, 0, 0, 1),
-        (edge_y, halo_y, 1, 0, -1),
-        (edge_x, halo_x, 0, 1, 0),
-        (edge_x, halo_x, 1, -1, 0),
-    )
-
-    def side_copy(index):
-        edge, _, side, dx, dy = sides[index]
-        return pltpu.make_async_remote_copy(
-            src_ref=edge.at[side],
-            dst_ref=edge.at[side + 2],
-            send_sem=edge_sems.at[0, index],
-            recv_sem=edge_sems.at[1, index],
-            device_id=(gx + dx, gy + dy),
-            device_id_type=MESH,
-        )
-
-    for index, (_, _, _, dx, dy) in enumerate(sides):
-
-        @pl.when(exists(gx + dx, gy + dy, nx, ny))
+    def accept_in_turn(i, carry):
+        k = lax.rem(i + 6, 8)
+
+        @pl.when(comes_in(k))
         def _():
-            side_copy(index).start()
-
-    for index, (edge, halo, side, dx, dy) in enumerate(sides):
-        there = exists(gx - dx, gy - dy, nx, ny)
-
-        @pl.when(there)
+            accept(k)
+
+        return carry
+
+    lax.fori_loop(0, 8, accept_in_turn, 0)
+
+    pack_edges(remapped, edge_y, edge_x)
+    each_side(lambda index: side_copy(index, *edges).start(), 1)
+
+    each_side(lambda index: side_copy(index, *flow).wait_recv(), -1)
+    for index, (side, dx, dy) in enumerate(sides):
+        edge = flow_y if dx == 0 else flow_x
+
+        @pl.when(jnp.logical_not(exists(gx - dx, gy - dy, nx, ny)))
         def _():
-            side_copy(index).wait_recv()
-            halo[side] = edge[side + 2]
-
-        @pl.when(jnp.logical_not(there))
-        def _():
-            halo[side] = jnp.zeros(halo.shape[1:], jnp.float32)
-
-    for index, (_, _, _, dx, dy) in enumerate(sides):
-
-        @pl.when(exists(gx + dx, gy + dy, nx, ny))
-        def _():
-            side_copy(index).wait_send()
+            edge[side + 2] = jnp.zeros(edge.shape[1:], jnp.float32)
+
+    def step(b, carry):
+        step_block(b, rows // 32, remapped, vel, flow_y, flow_x, out)
+        return carry
+
+    lax.fori_loop(0, rows // 32, step, 0)
+
+    def add_side(index):
+        side_copy(index, *edges).wait_recv()
+        side, dx, dy = sides[index]
+        bound = jnp.maximum if side == 0 else jnp.minimum
+        scale = time_step if side == 0 else -time_step
+        if dx != 0:
+            row = 0 if side == 0 else rows - 1
+            speed = scale * bound(vel[0, row : row + 1, :], 0.0)
+            for c in range(state_count):
+                out[c, row : row + 1, :] += speed * edge_x[side + 2, c : c + 1, :]
+            return
+        lane = 0 if side == 0 else 127
+
+        def add_block(b, carry):
+            span = pl.ds(pl.multiple_of(32 * b, 32), 32)
+            speed = jnp.where(lanes == lane, scale * bound(vel[1, span, :], 0.0), 0.0)
+            pack = pltpu.roll(edge_y[side + 2], lax.rem(128 + lane - 16 * b, 128), 1)
+            for c in range(state_count):
+                out[c, span, :] += speed * pltpu.roll(pack, (128 - c) % 128, 1)
+            return carry
+
+        lax.fori_loop(0, rows // 32, add_block, 0)
+
+    each_side(add_side, -1)
+    each_side(lambda index: side_copy(index, *flow).wait_send(), 1)
+    each_side(lambda index: side_copy(index, *edges).wait_send(), 1)
 
     def finish(k):
         label_copy(k).wait_send()
@@ -462,15 +500,14 @@
         functools.partial(exchange_kernel, nx, ny, caps),
         out_shape=(
             jax.ShapeDtypeStruct((state_count, rows, 128), f32),
-            jax.ShapeDtypeStruct((2, 32, 128), f32),
-            jax.ShapeDtypeStruct((2, 16, 128), f32),
             jax.ShapeDtypeStruct((1, 128), f32),
         ),
         in_specs=[pl.BlockSpec(memory_space=pltpu.SMEM)]
         + [in_vmem] * 4
         + [pl.BlockSpec(memory_space=pl.ANY)],
-        out_specs=(in_vmem,) * 4,
+        out_specs=(in_vmem,) * 2,
         scratch_shapes=[
+            vmem((state_count, rows, 128), f32),
             vmem((old.shape[1], 16, 128), f32),
             vmem(weights.shape, jnp.bfloat16),
             vmem((9, cap, state_count * 128), jnp.bfloat16),
@@ -479,12 +516,15 @@
             vmem((16 * CHUNK, 128), f32),
             vmem((4, 32, 128), f32),
             vmem((4, 16, 128), f32),
+            vmem((4, 32, 128), f32),
+            vmem((4, 16, 128), f32),
             vmem((3, 1, 128), f32),
             vmem((nx + ny, 1, 128), f32),
             dma((4,)),
             dma((2, 8)),
             dma((8, cap // CHUNK)),
             dma((8, cap // CHUNK)),
+            dma((2, 4)),
             dma((2, 4)),
             dma((2, nx + ny)),
         ],
@@ -499,33 +539,35 @@
     )(picks, labels, over, old, velocity, weights)
 
 
-def step_kernel(state, halo_y, halo_x, vel, out):
-    b = pl.program_id(0)
-    blocks = pl.num_programs(0)
-    states, rows, depth = state.shape[0], state.shape[1], 32
+def step_block(b, blocks, state, vel, flow_y, flow_x, out):
+    rows, depth = state.shape[1], 32
     base = pl.multiple_of(b * depth, depth)
+    span = pl.ds(base, depth)
     lane = lax.broadcasted_iota(jnp.int32, (depth, 128), 1)
     row = lax.broadcasted_iota(jnp.int32, (depth, 128), 0)
-    left_pack = pltpu.roll(halo_y[0], lax.rem(128 - 16 * b, 128), 1)
-    right_pack = pltpu.roll(halo_y[1], lax.rem(128 + 127 - 16 * b, 128), 1)
-
-    def around(ref, index, c):
-        mid = ref[index, pl.ds(base, depth), :]
-        above = jnp.where(b == 0, halo_x[0, c : c + 1, :], ref[index, pl.ds(jnp.maximum(base - 1, 0), 1), :])
-        below = jnp.where(
-            b == blocks - 1,
-            halo_x[1, c : c + 1, :],
-            ref[index, pl.ds(jnp.minimum(base + depth, rows - 1), 1), :],
-        )
+    left_pack = pltpu.roll(flow_y[2], lax.rem(128 - 16 * b, 128), 1)
+    right_pack = pltpu.roll(flow_y[3], lax.rem(128 + 127 - 16 * b, 128), 1)
+
+    def around(ref, c, halo):
+        mid = ref[c, span, :]
+        above = ref[c, pl.ds(jnp.maximum(base - 1, 0), 1), :]
+        below = ref[c, pl.ds(jnp.minimum(base + depth, rows - 1), 1), :]
+        if halo:
+            first, last = flow_x[2, c : c + 1, :], flow_x[3, c : c + 1, :]
+            shift = (128 - c) % 128
+            left, right = pltpu.roll(left_pack, shift, 1), pltpu.roll(right_pack, shift, 1)
+        else:
+            first = last = left = right = 0.0
+        above = jnp.where(b == 0, first, above)
+        below = jnp.where(b == blocks - 1, last, below)
         before_x = jnp.where(row == 0, above, pltpu.roll(mid, 1, 0))
         after_x = jnp.where(row == depth - 1, below, pltpu.roll(mid, depth - 1, 0))
-        shift = (128 - c) % 128
-        before_y = jnp.where(lane == 0, pltpu.roll(left_pack, shift, 1), pltpu.roll(mid, 1, 1))
-        after_y = jnp.where(lane == 127, pltpu.roll(right_pack, shift, 1), pltpu.roll(mid, 127, 1))
+        before_y = jnp.where(lane == 0, left, pltpu.roll(mid, 1, 1))
+        after_y = jnp.where(lane == 127, right, pltpu.roll(mid, 127, 1))
         return mid, before_x, after_x, before_y, after_y
 
-    u_x, ux_bx, ux_ax, ux_by, ux_ay = around(vel, 0, states)
-    u_y, uy_bx, uy_ax, uy_by, uy_ay = around(vel, 1, states + 1)
+    u_x, ux_bx, ux_ax, ux_by, ux_ay = around(vel, 0, True)
+    u_y, uy_bx, uy_ax, uy_by, uy_ay = around(vel, 1, True)
     d_xx = 0.5 * (ux_ax - ux_bx)
     l_xy = 0.5 * (ux_ay - ux_by)
     l_yx = 0.5 * (uy_ax - uy_bx)
@@ -538,7 +580,7 @@
     shear = (2.0 * interaction) * jnp.sqrt(
         2.0 * (d_xx * d_xx + d_yy * d_yy + d_zz * d_zz + 2.0 * (d_xy * d_xy)) + 1.0
     )
-    a_xx, a_yy, a_zz, a_xy, a_xz, a_yz = (state[c, pl.ds(base, depth), :] for c in range(6))
+    a_xx, a_yy, a_zz, a_xy, a_xz, a_yz = (state[c, span, :] for c in range(6))
     contraction = d_xx * a_xx + d_yy * a_yy + d_zz * a_zz + 2.0 * (d_xy * a_xy)
     fade = shape_factor * 2.0 * contraction + 3.0 * shear
     stress = 2.0 * shear_modulus
@@ -560,27 +602,14 @@
         stress * (d_xy + pull * a_xy),
     )
     for c, source in enumerate(sources):
-        mid, before_x, after_x, before_y, after_y = around(state, c, c)
+        mid, before_x, after_x, before_y, after_y = around(state, c, False)
         upwind = (
             plus_x * (mid - before_x)
             + minus_x * (after_x - mid)
             + plus_y * (mid - before_y)
             + minus_y * (after_y - mid)
         )
-        out[c] = mid + time_step * (source - upwind)
-
-
-def advance(state, halo_y, halo_x, velocity):
-    in_vmem = pl.BlockSpec(memory_space=pltpu.VMEM)
-    states, rows, width = state.shape
-    return pl.pallas_call(
-        step_kernel,
-        grid=(rows // 32,),
-        out_shape=jax.ShapeDtypeStruct(state.shape, jnp.float32),
-        in_specs=[in_vmem] * 4,
-        out_specs=pl.BlockSpec((states, 32, width), lambda b: (0, b, 0)),
-        compiler_params=pltpu.CompilerParams(vmem_limit_bytes=24 * MIB),
-    )(state, halo_y, halo_x, velocity)
+        out[c, span, :] = mid + time_step * (source - upwind)
 
 
 def per_device(
@@ -598,16 +627,12 @@
     lists = (send_count, source_block, tile_index, dest_device, dest_block)
     old = jnp.transpose(old_states, (1, 0, 2))
     places = plan(nx, ny, USUAL, lists)
-    *edges, any_over = exchange(nx, ny, USUAL, 0, *places, old, velocity, weight_tiles)
-
-    def again(*_):
-        *edges, _ = exchange(nx, ny, FULL, 1, *places, old, velocity, weight_tiles)
-        return advance(*edges, velocity)
-
-    def enough(*edges):
-        return advance(*edges, velocity)
-
-    states = lax.cond(any_over[0, 0] > 0, again, enough, *edges)
+    states, any_over = exchange(nx, ny, USUAL, 0, *places, old, velocity, weight_tiles)
+
+    def again(_):
+        return exchange(nx, ny, FULL, 1, *places, old, velocity, weight_tiles)[0]
+
+    states = lax.cond(any_over[0, 0] > 0, again, lambda enough: enough, states)
     return jnp.transpose(states, (1, 0, 2))
 
 

time: 50.1 us -> 48.9 us (0.976)
  Pallas kernels: 48 us -> 46.6 us
    pallas_call x1 -> x0, Pallas kernels: 2.92 us -> none  [advance(): pl.pallas_call(step_kernel, grid=(rows // 32,), out_shape=jax.ShapeDtypeS...]
    pallas_call x1, Pallas kernels: 43.8 us -> 45.3 us  [exchange(): pl.pallas_call(functools.partial(exchange_kernel, nx, ny, caps), out_shap...]
    unnamed x6 -> x5, local copies, waits for them, and re-layouts: 1.15 us -> 1.16 us
where the time goes in v5:
time: 48.9 us; the launch traced here: 48.5 us
  Pallas kernels  46.6 us (95%)
  local copies, waits for them, and re-layouts  1.16 us (2%)
  between operations  0.74 us (2%)
    pallas_call x1, Pallas kernels, exchange(): pl.pallas_call(functools.partial(exchange_kernel, nx, ny, caps), out_shap...  45.3 us
    pallas_call x1, Pallas kernels, plan(): pl.pallas_call(functools.partial(plan_kernel, nx, ny, caps), out_shape=(j...  1.27 us
    unnamed x5, local copies, waits for them, and re-layouts  1.16 us

profile of v5, /device:TPU:0, one launch (start us, length us, event | category | flops | bytes accessed | tf_op | source)
XLA Modules:
  0.0 48.5 jit_solution(14246197842577142646)
XLA Ops:
  0.7 1.3 %shard_map.82 = (s32[16,512]{1,0:T(8,128)S(1)}, s32[9,1,512]{2,1,0:T(1,128)S(1)}, f32[1,128]{1,0:T(1,128)S(1)}) custom-call(s32[1]{0:T(128)S(6)} %copy.12.send_count, s32[768]{0:T(1024)} %source_block.1, s32[768]{0:T(1024)} %tile_index.1, s32[768]{0:T(1024)} %dest_device.1, s32[768]{0:T(1024)} %dest_block.1), custom_call_target="tpu_custom_call" | custom-call | tf_op jit(solution)/shard_map/pallas_call | solution.py:122
  1.9 0.0 copy-start
  1.9 0.0 copy-start.1
  2.0 45.3 %shard_map.83 = (f32[12,256,128]{2,1,0:T(8,128)S(1)}, f32[1,128]{1,0:T(1,128)S(1)}) custom-call(s32[16,512]{1,0:T(8,128)S(1)} %get-tuple-element.33.picks, s32[9,1,512]{2,1,0:T(1,128)S(1)} %get-tuple-element.34.labels, f32[1,128]{1,0:T(1,128)S(1)} %get-tuple-element.35.over, bf16[12,128,128]{2,1,0:T(8,128)(2,1)} %bitcast.5, f32[2,256,128]{2,1,0:T(8,128)} %vel.1, ...), custom_call_target="tpu_custom_call" | custom-call | flops 905969664 | bytes 12582912 | tf_op jit(solution)/shard_map/pallas_call | solution.py:499
  47.3 0.0 copy-done
  47.4 0.0 copy-done.1
  47.4 1.1 %copy.13 = f32[256,12,128]{2,0,1:T(8,128)} copy(f32[256,12,128]{2,0,1:T(8,128)S(1)} %bitcast.7) | data formatting | bytes 3145728
  (1 shorter events, 0.0 us)
Async XLA Ops:
  1.9 45.4 %copy-start = (bf16[128,12,128]{2,0,1:T(8,128)(2,1)S(1)}, bf16[128,12,128]{2,0,1:T(8,128)(2,1)}, u32[]{:S(2)}) copy-start(bf16[128,12,128]{2,0,1:T(8,128)(2,1)} %param.10) | copy-start | bytes 1179652
  1.9 45.4 %copy-start.1 = (f32[2,256,128]{2,1,0:T(8,128)S(1)}, f32[2,256,128]{2,1,0:T(8,128)}, u32[]{:S(2)}) copy-start(f32[2,256,128]{2,1,0:T(8,128)} %vel.1) | copy-start | bytes 786436

commit v6 on v5

--- a/solution.py
+++ b/solution.py
@@ -282,14 +282,14 @@
 
     def pack_edges(ref, along_y, along_x):
         planes = ref.shape[0]
-        for side, lane in ((0, 127), (1, 0)):
+        for h in range(rows // 128):
             packed = jnp.zeros((32, 128), jnp.float32)
-            for b in range(rows // 32):
+            for q in range(4):
                 for c in range(planes):
-                    to = 16 * b + c
-                    moved = pltpu.roll(ref[c, pl.ds(32 * b, 32), :], (to - lane) % 128, 1)
-                    packed = jnp.where(lanes == to, moved, packed)
-            along_y[side] = packed
+                    to = 32 * q + 2 * c
+                    moved = pltpu.roll(ref[c, pl.ds(128 * h + 32 * q, 32), :], to + 1, 1)
+                    packed = jnp.where((lanes >> 1) == (to >> 1), moved, packed)
+            along_y[0, h] = packed
         for side, row in ((0, rows - 1), (1, 0)):
             for c in range(planes):
                 along_x[side, c : c + 1, :] = ref[c, row : row + 1, :]
@@ -298,8 +298,8 @@
         side, dx, dy = sides[index]
         edge = along_y if dx == 0 else along_x
         return pltpu.make_async_remote_copy(
-            src_ref=edge.at[side],
-            dst_ref=edge.at[side + 2],
+            src_ref=edge.at[0 if dx == 0 else side],
+            dst_ref=edge.at[side + 1 if dx == 0 else side + 2],
             send_sem=sems.at[0, index],
             recv_sem=sems.at[1, index],
             device_id=(gx + dx, gy + dy),
@@ -433,13 +433,20 @@
     pack_edges(remapped, edge_y, edge_x)
     each_side(lambda index: side_copy(index, *edges).start(), 1)
 
-    each_side(lambda index: side_copy(index, *flow).wait_recv(), -1)
-    for index, (side, dx, dy) in enumerate(sides):
-        edge = flow_y if dx == 0 else flow_x
-
-        @pl.when(jnp.logical_not(exists(gx - dx, gy - dy, nx, ny)))
-        def _():
-            edge[side + 2] = jnp.zeros(edge.shape[1:], jnp.float32)
+    def land(along_y, along_x, sems):
+        for index, (side, dx, dy) in enumerate(sides):
+            edge, slot = (along_y, side + 1) if dx == 0 else (along_x, side + 2)
+            there = exists(gx - dx, gy - dy, nx, ny)
+
+            @pl.when(there)
+            def _():
+                side_copy(index, along_y, along_x, sems).wait_recv()
+
+            @pl.when(jnp.logical_not(there))
+            def _():
+                edge[slot] = jnp.zeros(edge.shape[1:], jnp.float32)
+
+    land(*flow)
 
     def step(b, carry):
         step_block(b, rows // 32, remapped, vel, flow_y, flow_x, out)
@@ -447,32 +454,33 @@
 
     lax.fori_loop(0, rows // 32, step, 0)
 
-    def add_side(index):
-        side_copy(index, *edges).wait_recv()
-        side, dx, dy = sides[index]
-        bound = jnp.maximum if side == 0 else jnp.minimum
-        scale = time_step if side == 0 else -time_step
-        if dx != 0:
-            row = 0 if side == 0 else rows - 1
-            speed = scale * bound(vel[0, row : row + 1, :], 0.0)
-            for c in range(state_count):
-                out[c, row : row + 1, :] += speed * edge_x[side + 2, c : c + 1, :]
-            return
-        lane = 0 if side == 0 else 127
-
-        def add_block(b, carry):
-            span = pl.ds(pl.multiple_of(32 * b, 32), 32)
-            speed = jnp.where(lanes == lane, scale * bound(vel[1, span, :], 0.0), 0.0)
-            pack = pltpu.roll(edge_y[side + 2], lax.rem(128 + lane - 16 * b, 128), 1)
-            for c in range(state_count):
-                out[c, span, :] += speed * pltpu.roll(pack, (128 - c) % 128, 1)
-            return carry
-
-        lax.fori_loop(0, rows // 32, add_block, 0)
-
-    each_side(add_side, -1)
+    land(*edges)
+    for side, row in ((0, 0), (1, rows - 1)):
+        bound, scale = (jnp.maximum, time_step) if side == 0 else (jnp.minimum, -time_step)
+        speed = scale * bound(vel[0, row : row + 1, :], 0.0)
+        for c in range(state_count):
+            out[c, row : row + 1, :] += speed * edge_x[side + 2, c : c + 1, :]
+
+    each_side(lambda index: side_copy(index, *edges).wait_send(), 1)
+    for h in range(rows // 128):
+        moved = pltpu.roll(edge_y[1, h], 2, 1)
+        edge_y[0, h] = jnp.where((lanes & 1) == 0, moved, edge_y[2, h])
+
+    def add_block(b, carry):
+        span = pl.ds(pl.multiple_of(32 * b, 32), 32)
+        flow_here = vel[1, span, :]
+        speed = jnp.where(
+            lanes == 0,
+            time_step * jnp.maximum(flow_here, 0.0),
+            jnp.where(lanes == 127, -time_step * jnp.minimum(flow_here, 0.0), 0.0),
+        )
+        pack = pltpu.roll(edge_y[0, b // 4], lax.rem(128 + 126 - 32 * lax.rem(b, 4), 128), 1)
+        for c in range(state_count):
+            out[c, span, :] += speed * pltpu.roll(pack, (128 - 2 * c) % 128, 1)
+        return carry
+
+    lax.fori_loop(0, rows // 32, add_block, 0)
     each_side(lambda index: side_copy(index, *flow).wait_send(), 1)
-    each_side(lambda index: side_copy(index, *edges).wait_send(), 1)
 
     def finish(k):
         label_copy(k).wait_send()
@@ -514,9 +522,9 @@
             vmem((8, cap, state_count * 128), jnp.bfloat16),
             vmem((8, 1, 4 * WIDE), jnp.int32),
             vmem((16 * CHUNK, 128), f32),
-            vmem((4, 32, 128), f32),
+            vmem((3, rows // 128, 32, 128), f32),
             vmem((4, 16, 128), f32),
-            vmem((4, 32, 128), f32),
+            vmem((3, rows // 128, 32, 128), f32),
             vmem((4, 16, 128), f32),
             vmem((3, 1, 128), f32),
             vmem((nx + ny, 1, 128), f32),
@@ -545,8 +553,9 @@
     span = pl.ds(base, depth)
     lane = lax.broadcasted_iota(jnp.int32, (depth, 128), 1)
     row = lax.broadcasted_iota(jnp.int32, (depth, 128), 0)
-    left_pack = pltpu.roll(flow_y[2], lax.rem(128 - 16 * b, 128), 1)
-    right_pack = pltpu.roll(flow_y[3], lax.rem(128 + 127 - 16 * b, 128), 1)
+    quarter = 32 * lax.rem(b, 4)
+    left_pack = pltpu.roll(flow_y[1, b // 4], lax.rem(128 - quarter, 128), 1)
+    right_pack = pltpu.roll(flow_y[2, b // 4], lax.rem(128 + 126 - quarter, 128), 1)
 
     def around(ref, c, halo):
         mid = ref[c, span, :]
@@ -554,7 +563,7 @@
         below = ref[c, pl.ds(jnp.minimum(base + depth, rows - 1), 1), :]
         if halo:
             first, last = flow_x[2, c : c + 1, :], flow_x[3, c : c + 1, :]
-            shift = (128 - c) % 128
+            shift = (128 - 2 * c) % 128
             left, right = pltpu.roll(left_pack, shift, 1), pltpu.roll(right_pack, shift, 1)
         else:
             first = last = left = right = 0.0

time: 48.9 us -> 48.7 us (level)
  no operation moved by 1% of the time
where the time goes in v6:
time: 48.7 us; the launch traced here: 48.6 us
  Pallas kernels  46.7 us (96%)
  local copies, waits for them, and re-layouts  1.16 us (2%)
  between operations  0.74 us (2%)
    pallas_call x1, Pallas kernels, exchange(): pl.pallas_call(functools.partial(exchange_kernel, nx, ny, caps), out_shap...  45.4 us
    pallas_call x1, Pallas kernels, plan(): pl.pallas_call(functools.partial(plan_kernel, nx, ny, caps), out_shape=(j...  1.27 us
    unnamed x5, local copies, waits for them, and re-layouts  1.16 us

profile of v6, /device:TPU:0, one launch (start us, length us, event | category | flops | bytes accessed | tf_op | source)
XLA Modules:
  0.0 48.6 jit_solution(12829378420999551604)
XLA Ops:
  0.7 1.3 %shard_map.82 = (s32[16,512]{1,0:T(8,128)S(1)}, s32[9,1,512]{2,1,0:T(1,128)S(1)}, f32[1,128]{1,0:T(1,128)S(1)}) custom-call(s32[1]{0:T(128)S(6)} %copy.12.send_count, s32[768]{0:T(1024)} %source_block.1, s32[768]{0:T(1024)} %tile_index.1, s32[768]{0:T(1024)} %dest_device.1, s32[768]{0:T(1024)} %dest_block.1), custom_call_target="tpu_custom_call" | custom-call | tf_op jit(solution)/shard_map/pallas_call | solution.py:122
  1.9 0.0 copy-start
  1.9 0.0 copy-start.1
  2.0 45.4 %shard_map.83 = (f32[12,256,128]{2,1,0:T(8,128)S(1)}, f32[1,128]{1,0:T(1,128)S(1)}) custom-call(s32[16,512]{1,0:T(8,128)S(1)} %get-tuple-element.33.picks, s32[9,1,512]{2,1,0:T(1,128)S(1)} %get-tuple-element.34.labels, f32[1,128]{1,0:T(1,128)S(1)} %get-tuple-element.35.over, bf16[12,128,128]{2,1,0:T(8,128)(2,1)} %bitcast.5, f32[2,256,128]{2,1,0:T(8,128)} %vel.1, ...), custom_call_target="tpu_custom_call" | custom-call | flops 905969664 | bytes 12582912 | tf_op jit(solution)/shard_map/pallas_call | solution.py:507
  47.4 0.0 copy-done
  47.4 0.0 copy-done.1
  47.4 1.1 %copy.13 = f32[256,12,128]{2,0,1:T(8,128)} copy(f32[256,12,128]{2,0,1:T(8,128)S(1)} %bitcast.7) | data formatting | bytes 3145728
  (1 shorter events, 0.0 us)
Async XLA Ops:
  1.9 45.5 %copy-start = (bf16[128,12,128]{2,0,1:T(8,128)(2,1)S(1)}, bf16[128,12,128]{2,0,1:T(8,128)(2,1)}, u32[]{:S(2)}) copy-start(bf16[128,12,128]{2,0,1:T(8,128)(2,1)} %param.10) | copy-start | bytes 1179652
  1.9 45.5 %copy-start.1 = (f32[2,256,128]{2,1,0:T(8,128)S(1)}, f32[2,256,128]{2,1,0:T(8,128)}, u32[]{:S(2)}) copy-start(f32[2,256,128]{2,1,0:T(8,128)} %vel.1) | copy-start | bytes 786436

commit v7 on v6

--- a/solution.py
+++ b/solution.py
@@ -275,8 +275,6 @@
 
         lax.fori_loop(0, 8, step, 0)
 
-    each_channel(lambda k: label_copy(k).start(), goes_out)
-
     lanes = lax.broadcasted_iota(jnp.int32, (32, 128), 1)
     sides = ((0, 0, 1), (1, 0, -1), (0, 1, 0), (1, -1, 0))
 
@@ -315,8 +313,6 @@
 
     flow = (flow_y, flow_x, flow_sems)
     edges = (edge_y, edge_x, edge_sems)
-    pack_edges(vel, flow_y, flow_x)
-    each_side(lambda index: side_copy(index, *flow).start(), 1)
 
     blocks[...] = jnp.zeros_like(blocks)
     for c in range(state_count):
@@ -325,7 +321,7 @@
         span = pl.ds(part * depth, depth)
         pltpu.make_async_copy(weights.at[span], tiles.at[span], load_sem.at[part]).wait()
 
-    def compute_chunk(k, j):
+    def multiply(k, j, buffer):
         at = jnp.where(j < FIRST, j * CHUNK, (j - FIRST + 1) * WIDE)
         none = jnp.zeros((16, 128), jnp.bfloat16)
         join = jnp.concatenate
@@ -338,39 +334,66 @@
             piece = lax.dot_general(
                 left, right, (((1,), (1,)), ((), ())), preferred_element_type=jnp.float32
             )
-            turn[pl.ds(16 * i, 32), :] = piece[:32, :128]
-            turn[pl.ds(16 * i + 32, 32), :] = piece[32:, 128:]
+            turn[buffer, pl.ds(16 * i, 32), :] = piece[:32, :128]
+            turn[buffer, pl.ds(16 * i + 32, 32), :] = piece[32:, 128:]
+
+    def lay(k, j, buffer):
         for group in range(CHUNK // 16):
             for c in range(state_count):
-                turned = turn[pl.ds(256 * group + c, 16, stride=16), :]
+                turned = turn[buffer, pl.ds(256 * group + c, 16, stride=16), :]
                 outgoing[
                     k,
                     pl.ds(pl.multiple_of(j * CHUNK + 16 * group, 16), 16),
                     pl.ds(c * 128, 128),
                 ] = turned.astype(jnp.bfloat16)
 
+    def send(k, j):
+        @pl.when(k < 8)
+        def _():
+            chunk_copy(k, j).start()
+
     def sent(k):
         _, dy = step_of(k)
         return chunks_of(gx, gy, dy, nx, ny, caps)
 
     def channel(k, carry):
-        def chunk(j, carry):
-            compute_chunk(k, j)
-
+        def three(t, carry):
+            j = FIRST * t
+            multiply(k, j, 0)
+            multiply(k, j + 1, 1)
+            lay(k, j, 0)
+            send(k, j)
+            multiply(k, j + 2, 2)
+            lay(k, j + 1, 1)
+            send(k, j + 1)
+            lay(k, j + 2, 2)
+            send(k, j + 2)
+            return carry
+
+        def one(j, carry):
+            multiply(k, j, 0)
+            lay(k, j, 0)
+            send(k, j)
+            return carry
+
+        @pl.when((k == 8) | goes_out(k))
+        def _():
             @pl.when(k < 8)
             def _():
-                chunk_copy(k, j).start()
-
-            return carry
-
-        @pl.when((k == 8) | goes_out(k))
-        def _():
-            lax.fori_loop(0, jnp.where(k == 8, CHUNKS, sent(k)), chunk, 0)
+                label_copy(k).start()
+
+            lax.fori_loop(0, jnp.where(k == 8, CHUNKS // FIRST, 1), three, 0)
+            lax.fori_loop(FIRST, jnp.where(k == 8, FIRST, sent(k)), one, 0)
 
         @pl.when(k == 1)
         def _():
             gather_flag(0)
             send_flag(1)
+
+        @pl.when(k == 7)
+        def _():
+            pack_edges(vel, flow_y, flow_x)
+            each_side(lambda index: side_copy(index, *flow).start(), 1)
 
         return carry
 
@@ -466,20 +489,17 @@
         moved = pltpu.roll(edge_y[1, h], 2, 1)
         edge_y[0, h] = jnp.where((lanes & 1) == 0, moved, edge_y[2, h])
 
-    def add_block(b, carry):
-        span = pl.ds(pl.multiple_of(32 * b, 32), 32)
+    for b in range(rows // 32):
+        span = slice(32 * b, 32 * (b + 1))
         flow_here = vel[1, span, :]
         speed = jnp.where(
             lanes == 0,
             time_step * jnp.maximum(flow_here, 0.0),
             jnp.where(lanes == 127, -time_step * jnp.minimum(flow_here, 0.0), 0.0),
         )
-        pack = pltpu.roll(edge_y[0, b // 4], lax.rem(128 + 126 - 32 * lax.rem(b, 4), 128), 1)
+        pack = edge_y[0, b // 4]
         for c in range(state_count):
-            out[c, span, :] += speed * pltpu.roll(pack, (128 - 2 * c) % 128, 1)
-        return carry
-
-    lax.fori_loop(0, rows // 32, add_block, 0)
+            out[c, span, :] += speed * pltpu.roll(pack, (126 - 32 * (b % 4) - 2 * c) % 128, 1)
     each_side(lambda index: side_copy(index, *flow).wait_send(), 1)
 
     def finish(k):
@@ -521,7 +541,7 @@
             vmem((9, cap, state_count * 128), jnp.bfloat16),
             vmem((8, cap, state_count * 128), jnp.bfloat16),
             vmem((8, 1, 4 * WIDE), jnp.int32),
-            vmem((16 * CHUNK, 128), f32),
+            vmem((FIRST, 16 * CHUNK, 128), f32),
             vmem((3, rows // 128, 32, 128), f32),
             vmem((4, 16, 128), f32),
             vmem((3, rows // 128, 32, 128), f32),

time: 48.7 us -> 47.9 us (0.984)
  Pallas kernels: 46.7 us -> 45.9 us
    pallas_call x1, Pallas kernels: 45.4 us -> 44.6 us  [exchange(): pl.pallas_call(functools.partial(exchange_kernel, nx, ny, caps), out_shap...]
where the time goes in v7:
time: 47.9 us; the launch traced here: 47.8 us
  Pallas kernels  45.9 us (96%)
  local copies, waits for them, and re-layouts  1.16 us (2%)
  between operations  0.74 us (2%)
    pallas_call x1, Pallas kernels, exchange(): pl.pallas_call(functools.partial(exchange_kernel, nx, ny, caps), out_shap...  44.6 us
    pallas_call x1, Pallas kernels, plan(): pl.pallas_call(functools.partial(plan_kernel, nx, ny, caps), out_shape=(j...  1.27 us
    unnamed x5, local copies, waits for them, and re-layouts  1.16 us

profile of v7, /device:TPU:0, one launch (start us, length us, event | category | flops | bytes accessed | tf_op | source)
XLA Modules:
  0.0 47.8 jit_solution(12811073182944470899)
XLA Ops:
  0.7 1.3 %shard_map.82 = (s32[16,512]{1,0:T(8,128)S(1)}, s32[9,1,512]{2,1,0:T(1,128)S(1)}, f32[1,128]{1,0:T(1,128)S(1)}) custom-call(s32[1]{0:T(128)S(6)} %copy.12.send_count, s32[768]{0:T(1024)} %source_block.1, s32[768]{0:T(1024)} %tile_index.1, s32[768]{0:T(1024)} %dest_device.1, s32[768]{0:T(1024)} %dest_block.1), custom_call_target="tpu_custom_call" | custom-call | tf_op jit(solution)/shard_map/pallas_call | solution.py:122
  1.9 0.0 copy-start
  1.9 0.0 copy-start.1
  2.0 44.6 %shard_map.83 = (f32[12,256,128]{2,1,0:T(8,128)S(1)}, f32[1,128]{1,0:T(1,128)S(1)}) custom-call(s32[16,512]{1,0:T(8,128)S(1)} %get-tuple-element.33.picks, s32[9,1,512]{2,1,0:T(1,128)S(1)} %get-tuple-element.34.labels, f32[1,128]{1,0:T(1,128)S(1)} %get-tuple-element.35.over, bf16[12,128,128]{2,1,0:T(8,128)(2,1)} %bitcast.5, f32[2,256,128]{2,1,0:T(8,128)} %vel.1, ...), custom_call_target="tpu_custom_call" | custom-call | flops 905969664 | bytes 12582912 | tf_op jit(solution)/shard_map/pallas_call | solution.py:527
  46.6 0.0 copy-done
  46.6 0.0 copy-done.1
  46.6 1.1 %copy.13 = f32[256,12,128]{2,0,1:T(8,128)} copy(f32[256,12,128]{2,0,1:T(8,128)S(1)} %bitcast.7) | data formatting | bytes 3145728
  (1 shorter events, 0.0 us)
Async XLA Ops:
  1.9 44.7 %copy-start = (bf16[128,12,128]{2,0,1:T(8,128)(2,1)S(1)}, bf16[128,12,128]{2,0,1:T(8,128)(2,1)}, u32[]{:S(2)}) copy-start(bf16[128,12,128]{2,0,1:T(8,128)(2,1)} %param.10) | copy-start | bytes 1179652
  1.9 44.6 %copy-start.1 = (f32[2,256,128]{2,1,0:T(8,128)S(1)}, f32[2,256,128]{2,1,0:T(8,128)}, u32[]{:S(2)}) copy-start(f32[2,256,128]{2,1,0:T(8,128)} %vel.1) | copy-start | bytes 786436

commit v8 on v7

--- a/solution.py
+++ b/solution.py
@@ -197,6 +197,9 @@
 
     lax.fori_loop(1, nx, functools.partial(greet, along=along_gx), 0)
     lax.fori_loop(1, ny, functools.partial(greet, along=along_gy), 0)
+    blocks[...] = jnp.zeros_like(blocks)
+    for c in range(state_count):
+        blocks[:, c, :] = old[c].astype(jnp.float32)
     pl.semaphore_wait(barrier, neighbours_of(gx, gy, nx, ny) + nx + ny - 2)
 
     def flag_copy(turn_of, j):
@@ -232,7 +235,6 @@
         lax.fori_loop(1, (nx, ny)[turn_of], step, 0)
 
     flags[0] = over[...]
-    send_flag(0)
 
     def label_copy(k):
         dx, dy = step_of(k)
@@ -314,9 +316,6 @@
     flow = (flow_y, flow_x, flow_sems)
     edges = (edge_y, edge_x, edge_sems)
 
-    blocks[...] = jnp.zeros_like(blocks)
-    for c in range(state_count):
-        blocks[:, c, :] = old[c].astype(jnp.float32)
     for part in range(parts):
         span = pl.ds(part * depth, depth)
         pltpu.make_async_copy(weights.at[span], tiles.at[span], load_sem.at[part]).wait()
@@ -386,6 +385,10 @@
             lax.fori_loop(FIRST, jnp.where(k == 8, FIRST, sent(k)), one, 0)
 
         @pl.when(k == 1)
+        def _():
+            send_flag(0)
+
+        @pl.when(k == 3)
         def _():
             gather_flag(0)
             send_flag(1)

time: 47.9 us -> 47 us (0.981)
  Pallas kernels: 45.9 us -> 44.9 us
    pallas_call x1, Pallas kernels: 44.6 us -> 43.6 us  [exchange(): pl.pallas_call(functools.partial(exchange_kernel, nx, ny, caps), out_shap...]
where the time goes in v8:
time: 47 us; the launch traced here: 46.8 us
  Pallas kernels  44.9 us (96%)
  local copies, waits for them, and re-layouts  1.16 us (2%)
  between operations  0.74 us (2%)
    pallas_call x1, Pallas kernels, exchange(): pl.pallas_call(functools.partial(exchange_kernel, nx, ny, caps), out_shap...  43.6 us
    pallas_call x1, Pallas kernels, plan(): pl.pallas_call(functools.partial(plan_kernel, nx, ny, caps), out_shape=(j...  1.27 us
    unnamed x5, local copies, waits for them, and re-layouts  1.16 us

profile of v8, /device:TPU:0, one launch (start us, length us, event | category | flops | bytes accessed | tf_op | source)
XLA Modules:
  0.0 46.8 jit_solution(4386716544638782776)
XLA Ops:
  0.7 1.3 %shard_map.82 = (s32[16,512]{1,0:T(8,128)S(1)}, s32[9,1,512]{2,1,0:T(1,128)S(1)}, f32[1,128]{1,0:T(1,128)S(1)}) custom-call(s32[1]{0:T(128)S(6)} %copy.12.send_count, s32[768]{0:T(1024)} %source_block.1, s32[768]{0:T(1024)} %tile_index.1, s32[768]{0:T(1024)} %dest_device.1, s32[768]{0:T(1024)} %dest_block.1), custom_call_target="tpu_custom_call" | custom-call | tf_op jit(solution)/shard_map/pallas_call | solution.py:122
  1.9 0.0 copy-start
  1.9 0.0 copy-start.1
  2.0 43.6 %shard_map.83 = (f32[12,256,128]{2,1,0:T(8,128)S(1)}, f32[1,128]{1,0:T(1,128)S(1)}) custom-call(s32[16,512]{1,0:T(8,128)S(1)} %get-tuple-element.33.picks, s32[9,1,512]{2,1,0:T(1,128)S(1)} %get-tuple-element.34.labels, f32[1,128]{1,0:T(1,128)S(1)} %get-tuple-element.35.over, bf16[12,128,128]{2,1,0:T(8,128)(2,1)} %bitcast.5, f32[2,256,128]{2,1,0:T(8,128)} %vel.1, ...), custom_call_target="tpu_custom_call" | custom-call | flops 905969664 | bytes 12582912 | tf_op jit(solution)/shard_map/pallas_call | solution.py:530
  45.6 0.0 copy-done
  45.6 0.0 copy-done.1
  45.7 1.1 %copy.13 = f32[256,12,128]{2,0,1:T(8,128)} copy(f32[256,12,128]{2,0,1:T(8,128)S(1)} %bitcast.7) | data formatting | bytes 3145728
  (1 shorter events, 0.0 us)
Async XLA Ops:
  1.9 43.7 %copy-start = (bf16[128,12,128]{2,0,1:T(8,128)(2,1)S(1)}, bf16[128,12,128]{2,0,1:T(8,128)(2,1)}, u32[]{:S(2)}) copy-start(bf16[128,12,128]{2,0,1:T(8,128)(2,1)} %param.10) | copy-start | bytes 1179652
  1.9 43.7 %copy-start.1 = (f32[2,256,128]{2,1,0:T(8,128)S(1)}, f32[2,256,128]{2,1,0:T(8,128)}, u32[]{:S(2)}) copy-start(f32[2,256,128]{2,1,0:T(8,128)} %vel.1) | copy-start | bytes 786436

commit v9 on v8

--- a/solution.py
+++ b/solution.py
@@ -175,6 +175,19 @@
         pltpu.make_async_copy(weights.at[span], tiles.at[span], load_sem.at[part]).start()
 
     barrier = pltpu.get_barrier_semaphore()
+
+    def along_gx(j):
+        return (lax.rem(gx + j, nx), gy)
+
+    def along_gy(j):
+        return (gx, lax.rem(gy + j, ny))
+
+    def greet(j, carry, along):
+        pl.semaphore_signal(barrier, inc=1, device_id=along(j), device_id_type=MESH)
+        return carry
+
+    lax.fori_loop(1, ny, functools.partial(greet, along=along_gy), 0)
+    lax.fori_loop(1, nx, functools.partial(greet, along=along_gx), 0)
     for k in range(8):
         dx, dy = step_of(k)
 
@@ -184,19 +197,6 @@
                 barrier, inc=1, device_id=(gx + dx, gy + dy), device_id_type=MESH
             )
 
-
-    def along_gx(j):
-        return (lax.rem(gx + j, nx), gy)
-
-    def along_gy(j):
-        return (gx, lax.rem(gy + j, ny))
-
-    def greet(j, carry, along):
-        pl.semaphore_signal(barrier, inc=1, device_id=along(j), device_id_type=MESH)
-        return carry
-
-    lax.fori_loop(1, nx, functools.partial(greet, along=along_gx), 0)
-    lax.fori_loop(1, ny, functools.partial(greet, along=along_gy), 0)
     blocks[...] = jnp.zeros_like(blocks)
     for c in range(state_count):
         blocks[:, c, :] = old[c].astype(jnp.float32)
@@ -359,9 +359,9 @@
         def three(t, carry):
             j = FIRST * t
             multiply(k, j, 0)
-            multiply(k, j + 1, 1)
             lay(k, j, 0)
             send(k, j)
+            multiply(k, j + 1, 1)
             multiply(k, j + 2, 2)
             lay(k, j + 1, 1)
             send(k, j + 1)

time: 47 us -> 46.5 us (0.989)
  Pallas kernels: 44.9 us -> 44.4 us
    pallas_call x1, Pallas kernels: 43.6 us -> 43.1 us  [exchange(): pl.pallas_call(functools.partial(exchange_kernel, nx, ny, caps), out_shap...]
where the time goes in v9:
time: 46.5 us; the launch traced here: 46.3 us
  Pallas kernels  44.4 us (95%)
  local copies, waits for them, and re-layouts  1.16 us (2%)
  between operations  0.74 us (2%)
    pallas_call x1, Pallas kernels, exchange(): pl.pallas_call(functools.partial(exchange_kernel, nx, ny, caps), out_shap...  43.1 us
    pallas_call x1, Pallas kernels, plan(): pl.pallas_call(functools.partial(plan_kernel, nx, ny, caps), out_shape=(j...  1.27 us
    unnamed x5, local copies, waits for them, and re-layouts  1.16 us

profile of v9, /device:TPU:0, one launch (start us, length us, event | category | flops | bytes accessed | tf_op | source)
XLA Modules:
  0.0 46.3 jit_solution(2823253266038796117)
XLA Ops:
  0.7 1.3 %shard_map.82 = (s32[16,512]{1,0:T(8,128)S(1)}, s32[9,1,512]{2,1,0:T(1,128)S(1)}, f32[1,128]{1,0:T(1,128)S(1)}) custom-call(s32[1]{0:T(128)S(6)} %copy.12.send_count, s32[768]{0:T(1024)} %source_block.1, s32[768]{0:T(1024)} %tile_index.1, s32[768]{0:T(1024)} %dest_device.1, s32[768]{0:T(1024)} %dest_block.1), custom_call_target="tpu_custom_call" | custom-call | tf_op jit(solution)/shard_map/pallas_call | solution.py:122
  1.9 0.0 copy-start
  1.9 0.0 copy-start.1
  2.0 43.1 %shard_map.83 = (f32[12,256,128]{2,1,0:T(8,128)S(1)}, f32[1,128]{1,0:T(1,128)S(1)}) custom-call(s32[16,512]{1,0:T(8,128)S(1)} %get-tuple-element.33.picks, s32[9,1,512]{2,1,0:T(1,128)S(1)} %get-tuple-element.34.labels, f32[1,128]{1,0:T(1,128)S(1)} %get-tuple-element.35.over, bf16[12,128,128]{2,1,0:T(8,128)(2,1)} %bitcast.5, f32[2,256,128]{2,1,0:T(8,128)} %vel.1, ...), custom_call_target="tpu_custom_call" | custom-call | flops 905969664 | bytes 12582912 | tf_op jit(solution)/shard_map/pallas_call | solution.py:530
  45.1 0.0 copy-done
  45.1 0.0 copy-done.1
  45.1 1.1 %copy.13 = f32[256,12,128]{2,0,1:T(8,128)} copy(f32[256,12,128]{2,0,1:T(8,128)S(1)} %bitcast.7) | data formatting | bytes 3145728
  (1 shorter events, 0.0 us)
Async XLA Ops:
  1.9 43.2 %copy-start = (bf16[128,12,128]{2,0,1:T(8,128)(2,1)S(1)}, bf16[128,12,128]{2,0,1:T(8,128)(2,1)}, u32[]{:S(2)}) copy-start(bf16[128,12,128]{2,0,1:T(8,128)(2,1)} %param.10) | copy-start | bytes 1179652
  1.9 43.2 %copy-start.1 = (f32[2,256,128]{2,1,0:T(8,128)S(1)}, f32[2,256,128]{2,1,0:T(8,128)}, u32[]{:S(2)}) copy-start(f32[2,256,128]{2,1,0:T(8,128)} %vel.1) | copy-start | bytes 786436
